TPU v7x, 128 devices: a whole 4x4x4 slice. The times are simulated.
128 devices in a mesh: seq: 16 (over x, z_hi, core), ch: 8 (over z_lo, y).
Axes of the slice: x: 4, y: 4, z: 4 (z_hi: 2, z_lo: 2; z = z_hi * 2 + z_lo), core: 2. Of those that a mesh axis runs over, the one named last changes fastest.
Arguments:
- inputs: bfloat16 [1536, 131072], P('ch', 'seq'), may hold values from -6 to 6
- gating: bfloat16 [1536, 131072], P('ch', 'seq'), may hold values from -6 to 6
- upstream: bfloat16 [1536, 131072], P('ch', 'seq'), may hold values from -6 to 6
- factor_one: bfloat16 [512, 512], replicated, may hold values from -0.25 to 0.25
- factor_two: bfloat16 [256, 256], replicated, may hold values from -0.375 to 0.375
- factor_three: bfloat16 [256, 256], replicated, may hold values from -0.375 to 0.375
- factor_four: bfloat16 [512, 512], replicated, may hold values from -0.25 to 0.25
- kernel_cols: float32 [1536, 512], P('ch'), may hold values from -4 to 4
- kernel_rows: float32 [1536, 256], P('ch'), may hold values from -4 to 4
Outputs:
- input_grad: bfloat16 [1536, 131072], P('ch', 'seq')
- gating_grad: bfloat16 [1536, 131072], P('ch', 'seq')
- one_grad: float32 [512, 512], replicated
- two_grad: float32 [256, 256], replicated
- three_grad: float32 [256, 256], replicated
- four_grad: float32 [512, 512], replicated
- cols_grad: float32 [1536, 512], P('ch')
- rows_grad: float32 [1536, 256], P('ch')
All inputs are finite; a program needn't handle non-finite values.
Results may differ from a plain program's by a relative error of at most 0.0076.
Values may be sent and summed in bfloat16 or wider, within the bound.
No kernel may reach another device: no remote copies, remote signals or barrier semaphores. Data moves between devices by JAX's collectives and lax.ppermute only.
A program may use at most 128 MiB of HBM per device.

v0:
```python
import math

import jax
import jax.numpy as jnp
from jax import lax
from jax.sharding import PartitionSpec as P

P1 = 256
P2 = 512
C = 1536


def local(
    inputs,
    gating,
    upstream,
    factor_one,
    factor_two,
    factor_three,
    factor_four,
    kernel_cols,
    kernel_rows,
):
    width = inputs.shape[0]
    length = inputs.shape[1]
    flt = jnp.float32
    half = jnp.bfloat16
    rows_local = length // P2
    up_gate = (upstream.astype(flt) * gating.astype(flt)).astype(half)
    shaped = inputs.reshape(width, rows_local, P2)
    first_prod = jnp.einsum("cij,jk->cki", shaped, factor_one, preferred_element_type=flt)
    first_out = (first_prod * kernel_cols[:, :, None]).astype(half)
    columns = lax.all_to_all(first_out, "seq", split_axis=1, concat_axis=2, tiled=True)
    left_prod = jnp.einsum("ki,cji->cjk", factor_two, columns, preferred_element_type=flt)
    left_out = (left_prod * kernel_rows[:, None, :]).astype(half)
    second = jnp.einsum("ki,cji->cjk", factor_three, left_out, preferred_element_type=flt).astype(
        half
    )
    back_rows = lax.all_to_all(second, "seq", split_axis=2, concat_axis=1, tiled=True)
    gate_rows = up_gate.reshape(width, rows_local, P2)
    grad_four = jnp.einsum("cji,cik->jk", back_rows, gate_rows, preferred_element_type=flt)
    grad_second = jnp.einsum(
        "cik,jk->cji", gate_rows, factor_four, preferred_element_type=flt
    ).astype(half)
    grad_columns = lax.all_to_all(grad_second, "seq", split_axis=1, concat_axis=2, tiled=True)
    grad_three = jnp.einsum("cjk,cji->ki", grad_columns, left_out, preferred_element_type=flt)
    grad_left = jnp.einsum("ki,cjk->cji", factor_three, grad_columns, preferred_element_type=flt)
    rows_part = jnp.sum(grad_left * left_prod, axis=1)
    grad_prod = (grad_left * kernel_rows[:, None, :]).astype(half)
    grad_two = jnp.einsum("cjk,cji->ki", grad_prod, columns, preferred_element_type=flt)
    grad_first = jnp.einsum(
        "ki,cjk->cji", factor_two, grad_prod, preferred_element_type=flt
    ).astype(half)
    grad_back = lax.all_to_all(grad_first, "seq", split_axis=2, concat_axis=1, tiled=True)
    cols_part = jnp.sum(grad_back.astype(flt) * first_prod, axis=2)
    grad_inner = (grad_back.astype(flt) * kernel_cols[:, :, None]).astype(half)
    grad_one = jnp.einsum("cij,cki->jk", shaped, grad_inner, preferred_element_type=flt)
    input_grad = (
        jnp.einsum("cki,jk->cij", grad_inner, factor_one, preferred_element_type=flt)
        .astype(half)
        .reshape(width, length)
    )
    cols_sum, rows_sum = lax.psum((cols_part, rows_part), "seq")
    final_prod = jnp.einsum("cji,jk->cik", back_rows, factor_four, preferred_element_type=flt)
    gating_grad = (
        (upstream.reshape(width, rows_local, P2).astype(flt) * final_prod)
        .astype(half)
        .reshape(width, length)
    )
    one_sum, two_sum, three_sum, four_sum = lax.psum(
        (grad_one, grad_two, grad_three, grad_four), ("seq", "ch")
    )
    scale_one = 1.0 / math.sqrt(P1 * C)
    scale_two = 1.0 / math.sqrt(P2 * C)
    return (
        input_grad,
        gating_grad,
        one_sum * scale_one,
        two_sum * scale_two,
        three_sum * scale_two,
        four_sum * scale_one,
        cols_sum / math.sqrt(P1),
        rows_sum / math.sqrt(P2),
    )


def solution(mesh):
    in_specs = (
        P("ch", "seq"),
        P("ch", "seq"),
        P("ch", "seq"),
        P(),
        P(),
        P(),
        P(),
        P("ch", None),
        P("ch", None),
    )
    out_specs = (P("ch", "seq"), P("ch", "seq"), P(), P(), P(), P(), P("ch", None), P("ch", None))
    return jax.shard_map(local, mesh=mesh, in_specs=in_specs, out_specs=out_specs, check_vma=False)
```

profile of v0, /device:TPU:1, one launch (start us, length us, event | category | flops | bytes accessed | tf_op | source)
XLA Modules:
  0.0 642.5 jit_solution(8438789359948877841)
XLA Ops:
  7.2 4.0 multiply_convert_fusion.4
  17.6 8.2 %copy.93 = bf16[192,512,16]{0,2,1:T(8,128)(2,1)} copy(bf16[192,512,16]{1,2,0:T(8,128)(2,1)} %convert_bitcast_fusion.1) | data formatting | bytes 6291456 | tf_op jit(solution)/shard_map/convert_element_type | solution.py:44
  25.8 59.6 %all_to_all.63 = bf16[192,512,16]{0,2,1:T(8,128)(2,1)S(1)} all-to-all(bf16[192,512,16]{0,2,1:T(8,128)(2,1)} %copy.93), channel_id=1, replica_groups=mesh['seq'=16,'ch'=8] {'seq'}, dimensions={1} | all-to-all | bytes 6291456 | tf_op jit(solution)/shard_map/all_to_all | solution.py:45
  88.1 7.1 %copy.95 = bf16[192,32,256]{2,1,0:T(8,128)(2,1)} copy(bf16[192,32,256]{0,2,1:T(8,128)(2,1)} %bitcast.98) | data formatting | bytes 6291456 | tf_op jit(solution)/shard_map/all_to_all | solution.py:45
  103.4 8.2 %copy.96 = bf16[192,32,256]{0,1,2:T(8,128)(2,1)} copy(bf16[192,32,256]{2,1,0:T(8,128)(2,1)} %convolution_convert_fusion.1) | data formatting | bytes 6291456 | tf_op jit(solution)/shard_map/convert_element_type | solution.py:53
  111.6 55.8 %all_to_all.64 = bf16[192,32,256]{0,1,2:T(8,128)(2,1)S(1)} all-to-all(bf16[192,32,256]{0,1,2:T(8,128)(2,1)} %copy.96), channel_id=1, replica_groups=mesh['seq'=16,'ch'=8] {'seq'}, dimensions={2} | all-to-all | bytes 6291456 | tf_op jit(solution)/shard_map/all_to_all | solution.py:54
  173.0 4.3 copy.98
  177.3 9.5 %copy.99 = f32[192,512,16]{1,0,2:T(8,128)} copy(f32[192,512,16]{0,2,1:T(8,128)} %bitcast.97) | data formatting | bytes 12582912 | tf_op jit(solution)/shard_map/convert_element_type | solution.py:56
  186.9 7.4 %fusion.2 = (f32[192,512]{1,0:T(8,128)}, bf16[192,512,16]{1,0,2:T(8,128)(2,1)}, bf16[192,512,16]{1,0,2:T(8,128)(2,1)}) fusion(f32[192,512,16]{1,0,2:T(8,128)} %copy.99, f32[192,512]{1,0:T(8,128)S(1)} %copy-done.9, bf16[24,16,8,512]{3,2,1,0:T(8,128)(2,1)} %bitcast.104, bf16[512,512]{1,0:T(8,128)(2,1)S(1)} %copy-done), kind=kOutput, calls=%fused_computation.7 | convolution fusion | flops 1619951616 | bytes 17039360 | tf_op jit(solution)/shard_map/cij,jk->cki/dot_general | solution.py:31
  194.3 7.7 %copy.102 = bf16[192,512,16]{0,2,1:T(8,128)(2,1)} copy(bf16[192,512,16]{1,0,2:T(8,128)(2,1)} %get-tuple-element.49) | data formatting | bytes 6291456 | tf_op jit(solution)/shard_map/convert_element_type | solution.py:32
  202.0 5.9 all-to-all-start.2
  208.5 5.0 copy.130
  213.5 4.1 copy.128
  221.4 8.3 %copy.112 = bf16[192,512,16]{1,2,0:T(8,128)(2,1)} copy(bf16[192,512,16]{0,2,1:T(8,128)(2,1)} %bitcast.100) | data formatting | bytes 6291456 | tf_op jit(solution)/shard_map/convert_element_type | solution.py:56
  229.7 30.9 %all-to-all-done.2 = bf16[192,512,16]{0,2,1:T(8,128)(2,1)} async-done(((bf16[192,512,16]{0,2,1:T(8,128)(2,1)}), bf16[192,512,16]{0,2,1:T(8,128)(2,1)}, u32[]{:S(2)}, u32[]{:S(2)}) %all-to-all-start.2) | async-done | bytes 3145760 | tf_op jit(solution)/shard_map/all_to_all | solution.py:33
  260.6 4.7 copy.103
  265.3 7.1 %copy.104 = bf16[192,32,256]{2,1,0:T(8,128)(2,1)} copy(bf16[192,32,256]{0,2,1:T(8,128)(2,1)} %bitcast.101) | data formatting | bytes 6291456 | tf_op jit(solution)/shard_map/all_to_all | solution.py:33
  272.4 5.7 multiply_reduce_fusion
  282.4 8.2 %copy.105 = bf16[192,32,256]{0,1,2:T(8,128)(2,1)} copy(bf16[192,32,256]{2,1,0:T(8,128)(2,1)} %convolution_convert_fusion) | data formatting | bytes 6291456 | tf_op jit(solution)/shard_map/convert_element_type | solution.py:36
  290.6 12.4 %all-to-all-start.3 = ((bf16[192,32,256]{0,1,2:T(8,128)(2,1)}), bf16[192,32,256]{0,1,2:T(8,128)(2,1)}, u32[]{:S(2)}, u32[]{:S(2)}) async-start(bf16[192,32,256]{0,1,2:T(8,128)(2,1)} %copy.105), calls=%async_computation.3 | async-start | bytes 8388608 | tf_op jit(solution)/shard_map/all_to_all | solution.py:39
  303.1 5.6 convolution_bitcast_fusion.1
  309.0 5.6 convolution_bitcast_fusion.2
  314.9 4.5 fusion.13
  319.4 37.6 %all-to-all-done.3 = bf16[192,32,256]{0,1,2:T(8,128)(2,1)} async-done(((bf16[192,32,256]{0,1,2:T(8,128)(2,1)}), bf16[192,32,256]{0,1,2:T(8,128)(2,1)}, u32[]{:S(2)}, u32[]{:S(2)}) %all-to-all-start.3) | async-done | bytes 3145760 | tf_op jit(solution)/shard_map/all_to_all | solution.py:39
  357.0 7.0 %copy.107 = bf16[192,16,32,16]{0,3,2,1:T(8,128)(2,1)} copy(bf16[192,16,32,16]{0,2,3,1:T(8,128)(2,1)} %bitcast.17) | data formatting | bytes 6291456 | tf_op jit(solution)/shard_map/all_to_all | solution.py:39
  364.0 8.4 %copy.108 = bf16[192,512,16]{1,2,0:T(8,128)(2,1)} copy(bf16[192,512,16]{0,2,1:T(8,128)(2,1)} %bitcast.102) | data formatting | bytes 6291456 | tf_op jit(solution)/shard_map/all_to_all | solution.py:39
  372.4 5.7 convolution_bitcast_fusion
  378.1 4.2 fusion.10
  386.2 84.0 %all-reduce.7.cloned.1.call-done = (f32[192,512]{1,0:T(8,128)}, f32[192,256]{1,0:T(8,128)}) async-done(((f32[192,512]{1,0:T(8,128)}, f32[192,256]{1,0:T(8,128)}), (f32[192,512]{1,0:T(8,128)}, f32[192,256]{1,0:T(8,128)})) %all-reduce.7.cloned.1.call-update) | async-done | bytes 589840 | tf_op jit(solution)/shard_map/psum | solution.py:63
  473.5 5.5 fusion
  479.1 3.9 copy.129
  483.0 147.0 %all-reduce.5.cloned.1.call-done = (f32[512,512]{0,1:T(8,128)}, f32[256,256]{1,0:T(8,128)}, f32[256,256]{1,0:T(8,128)}, f32[512,512]{0,1:T(8,128)}) async-done(((f32[512,512]{0,1:T(8,128)}, f32[256,256]{1,0:T(8,128)}, f32[256,256]{1,0:T(8,128)}, f32[512,512]{0,1:T(8,128)}), (f32[512,512]{0,1:T(8,128)}, f32[256,256]{1,0:T(8,128)}, f32[256,256]{1,0:T(8,128)}, ...) | async-done | bytes 2621456 | tf_op jit(solution)/shard_map/psum | solution.py:70
  (55 shorter events, 44.5 us)
Async XLA Ops:
  7.2 179.7 %copy-start = (bf16[512,512]{1,0:T(8,128)(2,1)S(1)}, bf16[512,512]{1,0:T(8,128)(2,1)}, u32[]{:S(2)}) copy-start(bf16[512,512]{1,0:T(8,128)(2,1)} %param.12) | copy-start | bytes 1572868
  11.2 3.0 copy-start.13
  12.5 1.6 copy-start.8
  88.1 7.1 %copy-start.12 = (bf16[256,256]{1,0:T(8,128)(2,1)S(1)}, bf16[256,256]{1,0:T(8,128)(2,1)}, u32[]{:S(2)}) copy-start(bf16[256,256]{1,0:T(8,128)(2,1)} %param.14) | copy-start | bytes 393220
  95.2 5.5 copy-start.10
  95.2 5.5 copy-start.11
  98.1 2.6 copy-start.1
  169.9 1.9 copy-start.2
  177.3 9.5 %copy-start.9 = (f32[192,512]{1,0:T(8,128)S(1)}, f32[192,512]{1,0:T(8,128)}, u32[]{:S(2)}) copy-start(f32[192,512]{1,0:T(8,128)} %param.16) | copy-start | bytes 1179652
  202.0 58.6 %all-to-all-start.2 = ((bf16[192,512,16]{0,2,1:T(8,128)(2,1)}), bf16[192,512,16]{0,2,1:T(8,128)(2,1)}, u32[]{:S(2)}, u32[]{:S(2)}) async-start(bf16[192,512,16]{0,2,1:T(8,128)(2,1)} %copy.102), calls=%async_computation.2 | async-start | bytes 8388608 | tf_op jit(solution)/shard_map/all_to_all | solution.py:33
  208.5 5.1 copy-start.7
  213.5 4.1 copy-start.3
  278.1 1.7 copy-start.5
  290.6 66.4 %all-to-all-start.3 = ((bf16[192,32,256]{0,1,2:T(8,128)(2,1)}), bf16[192,32,256]{0,1,2:T(8,128)(2,1)}, u32[]{:S(2)}, u32[]{:S(2)}) async-start(bf16[192,32,256]{0,1,2:T(8,128)(2,1)} %copy.105), calls=%async_computation.3 | async-start | bytes 8388608 | tf_op jit(solution)/shard_map/all_to_all | solution.py:39
  303.0 167.1 %all-reduce.7.cloned.1.call-start = ((), (), s32[]{:S(2)}) async-start(), calls=%async_computation.5 | async-start | bytes 1179648 | tf_op jit(solution)/shard_map/psum | solution.py:63
  308.7 321.2 %all-reduce.5.cloned.1.call-start = ((), (), s32[]{:S(2)}) async-start(), calls=%async_computation.4 | async-start | bytes 5242880 | tf_op jit(solution)/shard_map/psum | solution.py:70
  309.0 5.6 copy-start.4
  309.0 5.9 copy-start.6
  631.7 2.6 copy-start.14
  631.7 2.6 copy-start.15
Sparse Core Ops, SparseCore 0:
  308.9 161.2 all-reduce.6
  477.1 152.7 all-reduce.4
where the time goes:
time: 650 us; the launch traced here: 642 us
  waiting for transfers between devices  299 us (46%)
  local copies, waits for them, and re-layouts  126 us (19%)
  blocking collectives  115 us (18%)
  matrix products  56.1 us (9%)
  starting transfers between devices  18.7 us (3%)
  between operations  14.7 us (2%)
  other arithmetic  12.5 us (2%)
    psum x1, waiting for transfers between devices, local(): lax.psum((grad_one, grad_two, grad_three, grad_four), ('seq', 'ch'))  147 us
    psum x1, waiting for transfers between devices, local(): cols_sum, rows_sum = lax.psum((cols_part, rows_part), 'seq')  84 us
    all_to_all x1, blocking collectives, local(): lax.all_to_all(grad_second, 'seq', split_axis=1, concat_axis=2, tiled=True)  59.6 us
    all_to_all x1, blocking collectives, local(): lax.all_to_all(grad_first, 'seq', split_axis=2, concat_axis=1, tiled=True)  55.8 us
    all_to_all x1, waiting for transfers between devices, local(): lax.all_to_all(second, 'seq', split_axis=2, concat_axis=1, tiled=True)  37.6 us
    all_to_all x1, waiting for transfers between devices, local(): lax.all_to_all(first_out, 'seq', split_axis=1, concat_axis=2, tiled=True)  30.9 us
    unnamed x40, local copies, waits for them, and re-layouts  29.1 us
    convert_element_type x4, local copies, waits for them, and re-layouts, local(): grad_inner = (grad_back.astype(flt) * kernel_cols[:, :, None]).astype(half)  24.6 us
  transfers between devices with their start and end apart: 4, of which 4 were waited for; matrix products, arithmetic and copies ran while one was open for 12% of the time, Pallas kernels for 0%

commit v1 on v0

v1 whole, which is shorter than its diff:
```python
import math

import jax
import jax.numpy as jnp
from jax import lax
from jax.experimental import pallas as pl
from jax.experimental.pallas import tpu as pltpu
from jax.sharding import PartitionSpec as P

P1 = 256
P2 = 512
C = 1536
N_SEQ = 16
N_CH = 8
WIDTH = C // N_CH
OWNED = WIDTH // N_SEQ
ROWS = P1 // N_SEQ
LENGTH = ROWS * P2
BLOCK = 16
STEPS = WIDTH // BLOCK
PIECES = 8
HIGH_ONE = P2 // PIECES
HIGH_TWO = P1 // PIECES
PIECE_ROWS = 2 * HIGH_ONE + HIGH_TWO
AXES = ("seq", "ch")

flt = jnp.float32
half = jnp.bfloat16


def params():
    return pltpu.CompilerParams(vmem_limit_bytes=56 * 1024 * 1024)


def cost(flops, moved):
    return pl.CostEstimate(flops=int(flops), bytes_accessed=int(moved), transcendentals=0)


def nn(a, b):
    return lax.dot_general(a, b, (((1,), (0,)), ((), ())), preferred_element_type=flt)


def nt(a, b):
    return lax.dot_general(a, b, (((1,), (1,)), ((), ())), preferred_element_type=flt)


def tn(a, b):
    return lax.dot_general(a, b, (((0,), (0,)), ((), ())), preferred_element_type=flt)


def split_kernel(x_ref, out_ref):
    out_ref[...] = x_ref[...].reshape(out_ref.shape)


def gate_kernel(g_ref, z_ref, out_ref):
    prod = (g_ref[...].astype(flt) * z_ref[...].astype(flt)).astype(half)
    out_ref[...] = prod.reshape(out_ref.shape)


def join_kernel(x_ref, out_ref):
    out_ref[...] = x_ref[...].reshape(out_ref.shape)


def final_kernel(h_ref, g_ref, four_ref, out_ref):
    prod = nn(h_ref[...].reshape(BLOCK * ROWS, P2), four_ref[...])
    prod = prod.reshape(BLOCK, LENGTH)
    out_ref[...] = (g_ref[...].astype(flt) * prod).astype(half)


FLAT = pl.BlockSpec((BLOCK, LENGTH), lambda i: (i, 0))
MATS = pl.BlockSpec((BLOCK, ROWS, P2), lambda i: (i, 0, 0))
FLAT_SHAPE = jax.ShapeDtypeStruct((WIDTH, LENGTH), half)
MATS_SHAPE = jax.ShapeDtypeStruct((WIDTH, ROWS, P2), half)
SIZE = WIDTH * LENGTH * 2


def split(x):
    return pl.pallas_call(
        split_kernel, grid=(STEPS,), in_specs=[FLAT], out_specs=MATS, out_shape=MATS_SHAPE,
        compiler_params=params(), cost_estimate=cost(0, 2 * SIZE), name="split_rows",
    )(x)


def gate(g, z):
    return pl.pallas_call(
        gate_kernel, grid=(STEPS,), in_specs=[FLAT, FLAT], out_specs=MATS, out_shape=MATS_SHAPE,
        compiler_params=params(), cost_estimate=cost(0, 3 * SIZE), name="gate_rows",
    )(g, z)


def join(x):
    return pl.pallas_call(
        join_kernel, grid=(STEPS,), in_specs=[MATS], out_specs=FLAT, out_shape=FLAT_SHAPE,
        compiler_params=params(), cost_estimate=cost(0, 2 * SIZE), name="join_rows",
    )(x)


def final(h, g, four):
    return pl.pallas_call(
        final_kernel, grid=(STEPS,),
        in_specs=[MATS, FLAT, pl.BlockSpec((P2, P2), lambda i: (0, 0))],
        out_specs=FLAT, out_shape=FLAT_SHAPE, compiler_params=params(),
        cost_estimate=cost(2 * WIDTH * LENGTH * P2, 3 * SIZE), name="final_rows",
    )(h, g, four)


def forward_kernel(x_ref, one_ref, two_ref, three_ref, kc_ref, kr_ref, h_ref):
    x = x_ref[...].reshape(P1, P2)
    first = (nn(x, one_ref[...]) * kc_ref[0]).astype(half)
    left = (nn(two_ref[...], first) * kr_ref[0]).astype(half)
    second = nn(three_ref[...], left).astype(half)
    h_ref[...] = second.reshape(h_ref.shape)


def backward_kernel(
    x_ref, e_ref, one_ref, two_ref, three_ref, four_ref, two_t_ref, three_t_ref, kc_ref, kr_ref,
    dx_ref, cols_ref, rows_ref, grads_ref, acc_one, acc_two, acc_three, acc_four,
):
    step = pl.program_id(0)
    kc = kc_ref[0]
    kr = kr_ref[0]
    x = x_ref[...].reshape(P1, P2)
    e = e_ref[...].reshape(P1, P2)
    first_prod = nn(x, one_ref[...])
    first = (first_prod * kc).astype(half)
    left_prod = nn(two_ref[...], first)
    left = (left_prod * kr).astype(half)
    second = nn(three_ref[...], left).astype(half)
    d_second = nt(e, four_ref[...]).astype(half)
    d_left = nn(three_t_ref[...], d_second)
    rows_ref[0] = jnp.sum(d_left * left_prod, axis=1, keepdims=True)
    d_prod = (d_left * kr).astype(half)
    d_first = nn(two_t_ref[...], d_prod).astype(half).astype(flt)
    cols_ref[0] = jnp.sum(d_first * first_prod, axis=0, keepdims=True)
    d_inner = (d_first * kc).astype(half)
    dx_ref[...] = nt(d_inner, one_ref[...]).astype(half).reshape(dx_ref.shape)

    @pl.when(step == 0)
    def _():
        acc_one[...] = jnp.zeros_like(acc_one)
        acc_two[...] = jnp.zeros_like(acc_two)
        acc_three[...] = jnp.zeros_like(acc_three)
        acc_four[...] = jnp.zeros_like(acc_four)

    acc_four[...] += tn(second, e)
    acc_three[...] += nt(d_second, left)
    acc_two[...] += nt(d_prod, first)
    acc_one[...] += tn(x, d_inner)

    @pl.when(step == OWNED - 1)
    def _():
        for p in range(PIECES):
            wide = slice(p * HIGH_ONE, (p + 1) * HIGH_ONE)
            tall = slice(p * HIGH_TWO, (p + 1) * HIGH_TWO)
            grads_ref[p, 0:HIGH_ONE, :] = acc_one[wide, :]
            grads_ref[p, HIGH_ONE : HIGH_ONE + HIGH_TWO, 0:P1] = acc_two[tall, :]
            grads_ref[p, HIGH_ONE : HIGH_ONE + HIGH_TWO, P1 : 2 * P1] = acc_three[tall, :]
            grads_ref[p, HIGH_ONE + HIGH_TWO : PIECE_ROWS, :] = acc_four[wide, :]


def whole(*shape):
    return pl.BlockSpec(shape, lambda q: (0,) * len(shape))


OWN = pl.BlockSpec((N_SEQ, 1, ROWS, P2), lambda q: (0, q, 0, 0))
OWN_SHAPE = jax.ShapeDtypeStruct((N_SEQ, OWNED, ROWS, P2), half)
COL = pl.BlockSpec((1, 1, P2), lambda q: (q, 0, 0))
ROW = pl.BlockSpec((1, P1, 1), lambda q: (q, 0, 0))
BIG = 2 * P1 * P2 * P2 * OWNED
SMALL = 2 * P1 * P1 * P2 * OWNED


def forward(x, one, two, three, kc, kr):
    return pl.pallas_call(
        forward_kernel, grid=(OWNED,),
        in_specs=[OWN, whole(P2, P2), whole(P1, P1), whole(P1, P1), COL, ROW],
        out_specs=OWN, out_shape=OWN_SHAPE, compiler_params=params(),
        cost_estimate=cost(BIG + 2 * SMALL, 2 * SIZE), name="forward_owned",
    )(x, one, two, three, kc, kr)


def backward(x, e, one, two, three, four, two_t, three_t, kc, kr):
    return pl.pallas_call(
        backward_kernel, grid=(OWNED,),
        in_specs=[
            OWN, OWN, whole(P2, P2), whole(P1, P1), whole(P1, P1), whole(P2, P2),
            whole(P1, P1), whole(P1, P1), COL, ROW,
        ],
        out_specs=[OWN, COL, ROW, whole(PIECES, PIECE_ROWS, P2)],
        out_shape=[
            OWN_SHAPE,
            jax.ShapeDtypeStruct((OWNED, 1, P2), flt),
            jax.ShapeDtypeStruct((OWNED, P1, 1), flt),
            jax.ShapeDtypeStruct((PIECES, PIECE_ROWS, P2), flt),
        ],
        scratch_shapes=[
            pltpu.VMEM((P2, P2), flt), pltpu.VMEM((P1, P1), flt),
            pltpu.VMEM((P1, P1), flt), pltpu.VMEM((P2, P2), flt),
        ],
        compiler_params=params(),
        cost_estimate=cost(5 * BIG + 6 * SMALL, 3 * SIZE), name="backward_owned",
    )(x, e, one, two, three, four, two_t, three_t, kc, kr)


def swap_pairs(x=0, zh=0, core=0, zl=0, y=0):
    flip_seq = x * 4 + zh * 2 + core
    flip_ch = zl * 4 + y
    return [
        (s * N_CH + c, (s ^ flip_seq) * N_CH + (c ^ flip_ch))
        for s in range(N_SEQ)
        for c in range(N_CH)
    ]


def swap(v, **flips):
    return lax.ppermute(v, AXES, swap_pairs(**flips))


def pick(v, index):
    return lax.dynamic_index_in_dim(v, index, 0, keepdims=False)


def in_order(bit, mine, theirs):
    return jnp.where(bit == 0, jnp.stack([mine, theirs]), jnp.stack([theirs, mine]))


def four_in_order(place, own, near, far, other):
    low = in_order(place & 1, own, near)
    high = in_order(place & 1, far, other)
    return in_order(place >> 1, low, high).reshape(4, *own.shape)


def sum_over_four(v, axes):
    v = v.astype(half)
    one, two, three = (swap(v, **flips) for flips in axes)
    return (v.astype(flt) + one.astype(flt)) + (two.astype(flt) + three.astype(flt))


def reduce_grads(grads, core, y):
    parts = grads.reshape(2, 4, PIECE_ROWS, P2)
    kept = pick(parts, core) + swap(pick(parts, 1 - core).astype(half), core=1).astype(flt)
    got = [swap(pick(kept, y ^ d).astype(half), y=d).astype(flt) for d in (1, 2, 3)]
    mine = pick(kept, y) + got[0] + got[1] + got[2]
    mine = sum_over_four(mine, [dict(x=1), dict(x=2), dict(x=3)])
    mine = sum_over_four(mine, [dict(zl=1), dict(zh=1), dict(zh=1, zl=1)]).astype(half)
    near, far, other = (swap(mine, y=d) for d in (1, 2, 3))
    mine = four_in_order(y, mine, near, far, other)
    both = in_order(core, mine, swap(mine, core=1))
    return both.reshape(PIECES, PIECE_ROWS, P2).astype(flt)


def gather_owned(v, x, zh, core):
    v = in_order(core, v, swap(v, core=1))
    v = in_order(zh, v, swap(v, zh=1))
    near, far, other = (swap(v, x=d) for d in (1, 2, 3))
    return four_in_order(x, v, near, far, other).reshape(WIDTH, P1 + P2)


def exchange(v):
    return lax.all_to_all(v, "seq", split_axis=0, concat_axis=0, tiled=True)


def local(
    inputs,
    gating,
    upstream,
    factor_one,
    factor_two,
    factor_three,
    factor_four,
    kernel_cols,
    kernel_rows,
):
    seq = lax.axis_index("seq")
    ch = lax.axis_index("ch")
    x_at, zh_at, core_at, y_at = seq >> 2, (seq >> 1) & 1, seq & 1, ch & 3
    owned = (N_SEQ, OWNED, ROWS, P2)
    kc = lax.dynamic_slice_in_dim(kernel_cols, seq * OWNED, OWNED, 0).reshape(OWNED, 1, P2)
    kr = lax.dynamic_slice_in_dim(kernel_rows, seq * OWNED, OWNED, 0).reshape(OWNED, P1, 1)

    x_own = exchange(split(inputs)).reshape(owned)
    e_own = exchange(gate(upstream, gating)).reshape(owned)
    h_own = forward(x_own, factor_one, factor_two, factor_three, kc, kr)
    h_rows = exchange(h_own.reshape(WIDTH, ROWS, P2))
    dx_own, cols, rows, grads = backward(
        x_own, e_own, factor_one, factor_two, factor_three, factor_four,
        factor_two.T, factor_three.T, kc, kr,
    )
    dx_rows = exchange(dx_own.reshape(WIDTH, ROWS, P2))
    gating_grad = final(h_rows, upstream, factor_four)
    input_grad = join(dx_rows)

    total = reduce_grads(grads, core_at, y_at)
    scale_one = 1.0 / math.sqrt(P1 * C)
    scale_two = 1.0 / math.sqrt(P2 * C)
    one_grad = total[:, 0:HIGH_ONE, :].reshape(P2, P2) * scale_one
    mid = total[:, HIGH_ONE : HIGH_ONE + HIGH_TWO, :].reshape(P1, P2) * scale_two
    four_grad = total[:, HIGH_ONE + HIGH_TWO : PIECE_ROWS, :].reshape(P2, P2) * scale_one

    owned_sums = jnp.concatenate([cols.reshape(OWNED, P2), rows.reshape(OWNED, P1)], axis=1)
    sums = gather_owned(owned_sums, x_at, zh_at, core_at)
    return (
        input_grad,
        gating_grad,
        one_grad,
        mid[:, 0:P1],
        mid[:, P1 : 2 * P1],
        four_grad,
        sums[:, 0:P2] / math.sqrt(P1),
        sums[:, P2 : P1 + P2] / math.sqrt(P2),
    )


def solution(mesh):
    in_specs = (
        P("ch", "seq"),
        P("ch", "seq"),
        P("ch", "seq"),
        P(),
        P(),
        P(),
        P(),
        P("ch", None),
        P("ch", None),
    )
    out_specs = (P("ch", "seq"), P("ch", "seq"), P(), P(), P(), P(), P("ch", None), P("ch", None))
    return jax.shard_map(local, mesh=mesh, in_specs=in_specs, out_specs=out_specs, check_vma=False)
```

time: 650 us -> 297 us (0.46)
  waiting for transfers between devices: 299 us -> 117 us
  blocking collectives: 115 us -> 0 us
  local copies, waits for them, and re-layouts: 126 us -> 16.5 us
  Pallas kernels: 0 us -> 78.5 us
  matrix products: 56.1 us -> 0 us
  starting transfers between devices: 18.7 us -> 61.9 us
  between operations: 14.7 us -> 0.81 us
    psum x2 -> x0, waiting for transfers between devices: 231 us -> none  [the longest x1 147 us: local(): lax.psum((grad_one, grad_two, grad_three, grad_four), ('seq', 'ch'))]
    all_to_all x2 -> x0, blocking collectives: 115 us -> none  [the longest x1 59.6 us: local(): lax.all_to_all(grad_second, 'seq', split_axis=1, concat_axis=2, tiled=True)]
    pallas_call x0 -> x6, Pallas kernels: none -> 78.5 us  [the longest x1 29.4 us: backward(): pl.pallas_call(backward_kernel, grid=(OWNED,), in_specs=[OWN, OWN, whole(...]
    dot_general x12 -> x0, matrix products: 56.1 us -> none  [the longest x1 7.43 us: local(): jnp.einsum('cij,jk->cki', shaped, factor_one, preferred_element_type=flt)]
    convert_element_type x8 -> x2, local copies, waits for them, and re-layouts: 56.9 us -> 2.31 us  [the longest x1 2.23 us: reduce_grads(): pick(parts, 1 - core).astype(half)]
    ppermute x0 -> x19, waiting for transfers between devices: none -> 52.6 us  [swap(): return lax.ppermute(v, AXES, swap_pairs(**flips))]
    all_to_all x7 -> x0, local copies, waits for them, and re-layouts: 39.5 us -> none  [the longest x2 15.5 us: local(): lax.all_to_all(second, 'seq', split_axis=2, concat_axis=1, tiled=True)]
    ppermute x0 -> x19, starting transfers between devices: none -> 28.6 us  [swap(): return lax.ppermute(v, AXES, swap_pairs(**flips))]
  transfers between devices with their start and end apart: 4 -> 23, of which waited for: 4 -> 7; matrix products, arithmetic and copies ran while one was open for 12% -> 10% of each run, Pallas kernels for 0% -> 10%
where the time goes in v1:
time: 297 us; the launch traced here: 293 us
  waiting for transfers between devices  117 us (39%)
  Pallas kernels  78.5 us (26%)
  starting transfers between devices  61.9 us (21%)
  other arithmetic  18.3 us (6%)
  local copies, waits for them, and re-layouts  16.5 us (6%)
    all_to_all x4, waiting for transfers between devices, exchange(): return lax.all_to_all(v, 'seq', split_axis=0, concat_axis=0, tiled=True)  64.3 us
    ppermute x19, waiting for transfers between devices, swap(): return lax.ppermute(v, AXES, swap_pairs(**flips))  52.6 us
    all_to_all x4, starting transfers between devices, exchange(): return lax.all_to_all(v, 'seq', split_axis=0, concat_axis=0, tiled=True)  33.3 us
    pallas_call x1, Pallas kernels, backward(): pl.pallas_call(backward_kernel, grid=(OWNED,), in_specs=[OWN, OWN, whole(...  29.4 us
    ppermute x19, starting transfers between devices, swap(): return lax.ppermute(v, AXES, swap_pairs(**flips))  28.6 us
    pallas_call x1, Pallas kernels, forward(): pl.pallas_call(forward_kernel, grid=(OWNED,), in_specs=[OWN, whole(P2, P2...  12.7 us
    pallas_call x1, Pallas kernels, final(): pl.pallas_call(final_kernel, grid=(STEPS,), in_specs=[MATS, FLAT, pl.Bloc...  11.1 us
    pallas_call x1, Pallas kernels, gate(): pl.pallas_call(gate_kernel, grid=(STEPS,), in_specs=[FLAT, FLAT], out_spe...  9.01 us
  transfers between devices with their start and end apart: 23, of which 7 were waited for; matrix products, arithmetic and copies ran while one was open for 10% of the time, Pallas kernels for 10%

profile of v1, /device:TPU:1, one launch (start us, length us, event | category | flops | bytes accessed | tf_op | source)
XLA Modules:
  0.0 292.8 jit_solution(8697725416596685203)
XLA Ops:
  0.6 8.2 %split_rows.1 = bf16[192,16,512]{2,1,0:T(8,128)(2,1)} custom-call(bf16[192,8192]{1,0:T(8,128)(2,1)} %x_ref.1), custom_call_target="tpu_custom_call" | custom-call | bytes 6291456 | tf_op jit(solution)/shard_map/split_rows/pallas_call | solution.py:78
  8.8 9.1 %all-to-all-start = ((bf16[192,16,512]{2,1,0:T(8,128)(2,1)}), bf16[192,16,512]{2,1,0:T(8,128)(2,1)S(1)}, u32[]{:S(2)}, u32[]{:S(2)}) async-start(bf16[192,16,512]{2,1,0:T(8,128)(2,1)} %split_rows.1), calls=%async_computation | async-start | bytes 6291456 | tf_op jit(solution)/shard_map/all_to_all | solution.py:260
  18.0 9.0 %gate_rows.1 = bf16[192,16,512]{2,1,0:T(8,128)(2,1)} custom-call(bf16[192,8192]{1,0:T(8,128)(2,1)} %g_ref.3, bf16[192,8192]{1,0:T(8,128)(2,1)} %z_ref.1), custom_call_target="tpu_custom_call" | custom-call | bytes 9437184 | tf_op jit(solution)/shard_map/gate_rows/pallas_call | solution.py:85
  27.0 30.7 %all-to-all-done = bf16[192,16,512]{2,1,0:T(8,128)(2,1)S(1)} async-done(((bf16[192,16,512]{2,1,0:T(8,128)(2,1)}), bf16[192,16,512]{2,1,0:T(8,128)(2,1)S(1)}, u32[]{:S(2)}, u32[]{:S(2)}) %all-to-all-start) | async-done | bytes 3145760 | tf_op jit(solution)/shard_map/all_to_all | solution.py:260
  59.4 9.4 %all-to-all-start.1 = ((bf16[192,16,512]{2,1,0:T(8,128)(2,1)}), bf16[192,16,512]{2,1,0:T(8,128)(2,1)}, u32[]{:S(2)}, u32[]{:S(2)}) async-start(bf16[192,16,512]{2,1,0:T(8,128)(2,1)} %gate_rows.1), calls=%async_computation.1 | async-start | bytes 6291456 | tf_op jit(solution)/shard_map/all_to_all | solution.py:260
  71.9 1.7 copy.19
  75.2 33.5 %all-to-all-done.1 = bf16[192,16,512]{2,1,0:T(8,128)(2,1)} async-done(((bf16[192,16,512]{2,1,0:T(8,128)(2,1)}), bf16[192,16,512]{2,1,0:T(8,128)(2,1)}, u32[]{:S(2)}, u32[]{:S(2)}) %all-to-all-start.1) | async-done | bytes 3145760 | tf_op jit(solution)/shard_map/all_to_all | solution.py:260
  108.7 29.4 %backward_owned.1 = (bf16[16,12,16,512]{3,2,1,0:T(8,128)(2,1)}, f32[12,1,512]{2,1,0:T(1,128)}, f32[12,256,1]{2,1,0:T(8,128)}, f32[8,160,512]{2,1,0:T(8,128)}) custom-call(bf16[16,12,16,512]{3,2,1,0:T(8,128)(2,1)} %bitcast.60, bf16[16,12,16,512]{3,2,1,0:T(8,128)(2,1)} %bitcast.1.e_ref, bf16[512,512]{1,0:T(8,128)(2,1)} %one_ref.3, bf16[256,256]{1,0:T(8,128)(2,1)} %two_ref.3, ...), custom_call_target="tpu_custom_call" | custom-call | flops 12884901888 | bytes 9437184 | tf_op jit(solution)/shard_map/backward_owned/pallas_call | solution.py:183
  138.1 9.5 %all-to-all-start.2 = ((bf16[192,16,512]{2,1,0:T(8,128)(2,1)}), bf16[192,16,512]{2,1,0:T(8,128)(2,1)S(1)}, u32[]{:S(2)}, u32[]{:S(2)}) async-start(bf16[192,16,512]{2,1,0:T(8,128)(2,1)} %bitcast.58), calls=%async_computation.2 | async-start | bytes 6291456 | tf_op jit(solution)/shard_map/all_to_all | solution.py:260
  147.6 2.2 fusion
  149.9 1.9 reduce
  152.3 1.7 bitcast_add_fusion
  155.6 2.6 collective-permute-start.2
  158.2 12.7 %forward_owned.1 = bf16[16,12,16,512]{3,2,1,0:T(8,128)(2,1)} custom-call(bf16[16,12,16,512]{3,2,1,0:T(8,128)(2,1)} %bitcast.61, bf16[512,512]{1,0:T(8,128)(2,1)} %one_ref.3, bf16[256,256]{1,0:T(8,128)(2,1)} %two_ref.3, bf16[256,256]{1,0:T(8,128)(2,1)} %three_ref.3, f32[12,1,512]{2,1,0:T(1,128)} %reshape.563.kc_ref, f32[12,256,1]{2,1,0:T(8,128)} %copy.21.kr_ref), custom_call_target="tpu_custom_call" | custom-call | flops 3221225472 | bytes 6291456 | tf_op jit(solution)/shard_map/forward_owned/pallas_call | solution.py:174
  172.4 2.4 collective-permute-start.5
  175.6 2.8 collective-permute-start.15
  179.1 9.3 %collective-permute-done.4 = bf16[160,512]{1,0:T(8,128)(2,1)S(1)} collective-permute-done((bf16[160,512]{1,0:T(8,128)(2,1)S(1)}, bf16[160,512]{1,0:T(8,128)(2,1)S(1)}, u32[]{:S(2)}, u32[]{:S(2)}) %collective-permute-start.4) | collective-permute-done | bytes 163872 | tf_op jit(solution)/shard_map/ppermute | solution.py:216
  188.4 9.2 %collective-permute-done.5 = bf16[160,512]{1,0:T(8,128)(2,1)S(1)} collective-permute-done((bf16[160,512]{1,0:T(8,128)(2,1)S(1)}, bf16[160,512]{1,0:T(8,128)(2,1)S(1)}, u32[]{:S(2)}, u32[]{:S(2)}) %collective-permute-start.5) | collective-permute-done | bytes 163872 | tf_op jit(solution)/shard_map/ppermute | solution.py:216
  198.5 3.1 %collective-permute-start.9 = (bf16[160,512]{1,0:T(8,128)(2,1)S(1)}, bf16[160,512]{1,0:T(8,128)(2,1)}, u32[]{:S(2)}, u32[]{:S(2)}) collective-permute-start(bf16[160,512]{1,0:T(8,128)(2,1)S(1)} %add_convert_fusion.1), channel_id=1, source_target_pairs={{0,20},{1,21},{2,22},{3,23},{4,16},{5,17},{6,18},{7,19},{8,28},{9,... | collective-permute-start | bytes 491528 | tf_op jit(solution)/shard_map/ppermute | solution.py:216
  204.0 5.2 %all-to-all-start.3 = ((bf16[192,16,512]{2,1,0:T(8,128)(2,1)}), bf16[192,16,512]{2,1,0:T(8,128)(2,1)S(1)}, u32[]{:S(2)}, u32[]{:S(2)}) async-start(bf16[192,16,512]{2,1,0:T(8,128)(2,1)} %bitcast.59), calls=%async_computation.3 | async-start | bytes 6291456 | tf_op jit(solution)/shard_map/all_to_all | solution.py:260
  211.8 2.4 collective-permute-start.17
  217.8 2.7 collective-permute-start.11
  220.5 29.7 %collective-permute-done.16 = f32[2,2,12,768]{3,2,1,0:T(8,128)S(1)} collective-permute-done((f32[2,2,12,768]{3,2,1,0:T(8,128)S(1)}, f32[2,2,12,768]{3,2,1,0:T(8,128)S(1)}, u32[]{:S(2)}, u32[]{:S(2)}) %collective-permute-start.16) | collective-permute-done | bytes 147488 | tf_op jit(solution)/shard_map/ppermute | solution.py:216
  250.1 2.7 collective-permute-start.12
  253.0 2.6 collective-permute-done.12
  256.6 2.4 collective-permute-start.13
  259.0 1.7 collective-permute-done.17
  261.7 2.0 select_n.205
  265.3 1.8 slice_multiply_fusion.3
  267.1 1.9 maximum_select_fusion
  271.9 8.2 %join_rows.1 = bf16[192,8192]{1,0:T(8,128)(2,1)} custom-call(bf16[192,16,512]{2,1,0:T(8,128)(2,1)} %copy-done.3), custom_call_target="tpu_custom_call" | custom-call | bytes 6291456 | tf_op jit(solution)/shard_map/join_rows/pallas_call | solution.py:92
  281.8 11.1 %final_rows.1 = bf16[192,8192]{1,0:T(8,128)(2,1)} custom-call(bf16[192,16,512]{2,1,0:T(8,128)(2,1)} %copy-done.2, bf16[192,8192]{1,0:T(8,128)(2,1)} %g_ref.3, bf16[512,512]{1,0:T(8,128)(2,1)} %four_ref.3), custom_call_target="tpu_custom_call" | custom-call | flops 1610612736 | bytes 9437184 | tf_op jit(solution)/shard_map/final_rows/pallas_call | solution.py:99
  (68 shorter events, 29.0 us)
Async XLA Ops:
  0.6 70.6 %copy-start = (f32[192,512]{1,0:T(8,128)S(1)}, f32[192,512]{1,0:T(8,128)}, u32[]{:S(2)}) copy-start(f32[192,512]{1,0:T(8,128)} %param.16) | copy-start | bytes 1179652
  8.8 48.9 %all-to-all-start = ((bf16[192,16,512]{2,1,0:T(8,128)(2,1)}), bf16[192,16,512]{2,1,0:T(8,128)(2,1)S(1)}, u32[]{:S(2)}, u32[]{:S(2)}) async-start(bf16[192,16,512]{2,1,0:T(8,128)(2,1)} %split_rows.1), calls=%async_computation | async-start | bytes 6291456 | tf_op jit(solution)/shard_map/all_to_all | solution.py:260
  57.7 1.7 copy-start.4
  59.4 49.3 %all-to-all-start.1 = ((bf16[192,16,512]{2,1,0:T(8,128)(2,1)}), bf16[192,16,512]{2,1,0:T(8,128)(2,1)}, u32[]{:S(2)}, u32[]{:S(2)}) async-start(bf16[192,16,512]{2,1,0:T(8,128)(2,1)} %gate_rows.1), calls=%async_computation.1 | async-start | bytes 6291456 | tf_op jit(solution)/shard_map/all_to_all | solution.py:260
  138.1 11.8 %copy-start.6 = (f32[12,1,512]{2,1,0:T(1,128)S(1)}, f32[12,1,512]{2,1,0:T(1,128)}, u32[]{:S(2)}) copy-start(f32[12,1,512]{2,1,0:T(1,128)} %get-tuple-element.14) | copy-start | bytes 73732
  138.1 64.2 %all-to-all-start.2 = ((bf16[192,16,512]{2,1,0:T(8,128)(2,1)}), bf16[192,16,512]{2,1,0:T(8,128)(2,1)S(1)}, u32[]{:S(2)}, u32[]{:S(2)}) async-start(bf16[192,16,512]{2,1,0:T(8,128)(2,1)} %bitcast.58), calls=%async_computation.2 | async-start | bytes 6291456 | tf_op jit(solution)/shard_map/all_to_all | solution.py:260
  149.8 2.5 collective-permute-start
  151.8 23.1 %collective-permute-start.14 = (f32[12,768]{1,0:T(8,128)S(1)}, f32[12,768]{1,0:T(8,128)S(1)}, u32[]{:S(2)}, u32[]{:S(2)}) collective-permute-start(f32[12,768]{1,0:T(8,128)S(1)} %get-tuple-element.25), channel_id=1, source_target_pairs={{0,8},{1,9},{2,10},{3,11},{4,12},{5,13},{6,14},{7,15},{8,0},{9,1},... | collective-permute-start | bytes 110600 | tf_op jit(solution)/shard_map/ppermute | solution.py:216
  154.1 16.7 %collective-permute-start.1 = (bf16[160,512]{1,0:T(8,128)(2,1)S(1)}, bf16[160,512]{1,0:T(8,128)(2,1)S(1)}, u32[]{:S(2)}, u32[]{:S(2)}) collective-permute-start(bf16[160,512]{1,0:T(8,128)(2,1)S(1)} %get-tuple-element.18), channel_id=1, source_target_pairs={{0,1},{1,0},{2,3},{3,2},{4,5},{5,4},{6,7},{7,6},{8,9},{9,8},{10,11... | collective-permute-start | bytes 491528 | tf_op jit(solution)/shard_map/ppermute | solution.py:216
  155.6 15.3 %collective-permute-start.2 = (bf16[160,512]{1,0:T(8,128)(2,1)S(1)}, bf16[160,512]{1,0:T(8,128)(2,1)S(1)}, u32[]{:S(2)}, u32[]{:S(2)}) collective-permute-start(bf16[160,512]{1,0:T(8,128)(2,1)S(1)} %get-tuple-element.20), channel_id=1, source_target_pairs={{0,2},{1,3},{2,0},{3,1},{4,6},{5,7},{6,4},{7,5},{8,10},{9,11},{10,... | collective-permute-start | bytes 491528 | tf_op jit(solution)/shard_map/ppermute | solution.py:216
  158.2 12.7 %collective-permute-start.3 = (bf16[160,512]{1,0:T(8,128)(2,1)S(1)}, bf16[160,512]{1,0:T(8,128)(2,1)S(1)}, u32[]{:S(2)}, u32[]{:S(2)}) collective-permute-start(bf16[160,512]{1,0:T(8,128)(2,1)S(1)} %get-tuple-element.19), channel_id=1, source_target_pairs={{0,3},{1,2},{2,1},{3,0},{4,7},{5,6},{6,5},{7,4},{8,11},{9,10},{10,... | collective-permute-start | bytes 491528 | tf_op jit(solution)/shard_map/ppermute | solution.py:216
  170.9 17.4 %collective-permute-start.4 = (bf16[160,512]{1,0:T(8,128)(2,1)S(1)}, bf16[160,512]{1,0:T(8,128)(2,1)S(1)}, u32[]{:S(2)}, u32[]{:S(2)}) collective-permute-start(bf16[160,512]{1,0:T(8,128)(2,1)S(1)} %fusion.3), channel_id=1, source_target_pairs={{0,32},{1,33},{2,34},{3,35},{4,36},{5,37},{6,38},{7,39},{8,40},{9,... | collective-permute-start | bytes 491528 | tf_op jit(solution)/shard_map/ppermute | solution.py:216
  172.4 25.2 %collective-permute-start.5 = (bf16[160,512]{1,0:T(8,128)(2,1)S(1)}, bf16[160,512]{1,0:T(8,128)(2,1)S(1)}, u32[]{:S(2)}, u32[]{:S(2)}) collective-permute-start(bf16[160,512]{1,0:T(8,128)(2,1)S(1)} %fusion.3), channel_id=1, source_target_pairs={{0,64},{1,65},{2,66},{3,67},{4,68},{5,69},{6,70},{7,71},{8,72},{9,... | collective-permute-start | bytes 491528 | tf_op jit(solution)/shard_map/ppermute | solution.py:216
  174.8 22.8 %collective-permute-start.6 = (bf16[160,512]{1,0:T(8,128)(2,1)S(1)}, bf16[160,512]{1,0:T(8,128)(2,1)S(1)}, u32[]{:S(2)}, u32[]{:S(2)}) collective-permute-start(bf16[160,512]{1,0:T(8,128)(2,1)S(1)} %fusion.3), channel_id=1, source_target_pairs={{0,96},{1,97},{2,98},{3,99},{4,100},{5,101},{6,102},{7,103},{8,104... | collective-permute-start | bytes 491528 | tf_op jit(solution)/shard_map/ppermute | solution.py:216
  175.6 33.6 %collective-permute-start.15 = (f32[2,12,768]{2,1,0:T(8,128)}, f32[2,12,768]{2,1,0:T(8,128)}, u32[]{:S(2)}, u32[]{:S(2)}) collective-permute-start(f32[2,12,768]{2,1,0:T(8,128)} %maximum_select_fusion.10), channel_id=1, source_target_pairs={{0,16},{1,17},{2,18},{3,19},{4,20},{5,21},{6,22},{7,23},{8,24},{9,... | collective-permute-start | bytes 221192 | tf_op jit(solution)/shard_map/ppermute | solution.py:216
  197.7 16.5 %collective-permute-start.7 = (bf16[160,512]{1,0:T(8,128)(2,1)S(1)}, bf16[160,512]{1,0:T(8,128)(2,1)}, u32[]{:S(2)}, u32[]{:S(2)}) collective-permute-start(bf16[160,512]{1,0:T(8,128)(2,1)S(1)} %add_convert_fusion.1), channel_id=1, source_target_pairs={{0,4},{1,5},{2,6},{3,7},{4,0},{5,1},{6,2},{7,3},{8,12},{9,13},{10,... | collective-permute-start | bytes 491528 | tf_op jit(solution)/shard_map/ppermute | solution.py:216
  198.5 15.7 %collective-permute-start.8 = (bf16[160,512]{1,0:T(8,128)(2,1)S(1)}, bf16[160,512]{1,0:T(8,128)(2,1)}, u32[]{:S(2)}, u32[]{:S(2)}) collective-permute-start(bf16[160,512]{1,0:T(8,128)(2,1)S(1)} %add_convert_fusion.1), channel_id=1, source_target_pairs={{0,16},{1,17},{2,18},{3,19},{4,20},{5,21},{6,22},{7,23},{8,24},{9,... | collective-permute-start | bytes 491528 | tf_op jit(solution)/shard_map/ppermute | solution.py:216
  198.5 15.7 %collective-permute-start.9 = (bf16[160,512]{1,0:T(8,128)(2,1)S(1)}, bf16[160,512]{1,0:T(8,128)(2,1)}, u32[]{:S(2)}, u32[]{:S(2)}) collective-permute-start(bf16[160,512]{1,0:T(8,128)(2,1)S(1)} %add_convert_fusion.1), channel_id=1, source_target_pairs={{0,20},{1,21},{2,22},{3,23},{4,16},{5,17},{6,18},{7,19},{8,28},{9,... | collective-permute-start | bytes 491528 | tf_op jit(solution)/shard_map/ppermute | solution.py:216
  202.3 1.7 copy-start.3
  202.3 14.5 %copy-start.5 = (f32[1,1,2,12,768]{4,3,2,1,0:T(8,128)S(1)}, f32[1,1,2,12,768]{4,3,2,1,0:T(8,128)}, u32[]{:S(2)}) copy-start(f32[1,1,2,12,768]{4,3,2,1,0:T(8,128)} %fusion.11) | copy-start | bytes 221188
  204.0 76.2 %all-to-all-start.3 = ((bf16[192,16,512]{2,1,0:T(8,128)(2,1)}), bf16[192,16,512]{2,1,0:T(8,128)(2,1)S(1)}, u32[]{:S(2)}, u32[]{:S(2)}) async-start(bf16[192,16,512]{2,1,0:T(8,128)(2,1)} %bitcast.59), calls=%async_computation.3 | async-start | bytes 6291456 | tf_op jit(solution)/shard_map/all_to_all | solution.py:260
  210.3 39.9 %collective-permute-start.16 = (f32[2,2,12,768]{3,2,1,0:T(8,128)S(1)}, f32[2,2,12,768]{3,2,1,0:T(8,128)S(1)}, u32[]{:S(2)}, u32[]{:S(2)}) collective-permute-start(f32[2,2,12,768]{3,2,1,0:T(8,128)S(1)} %maximum_select_fusion.8), channel_id=1, source_target_pairs={{0,32},{1,33},{2,34},{3,35},{4,36},{5,37},{6,38},{7,39},{8,40},{9,... | collective-permute-start | bytes 442376 | tf_op jit(solution)/shard_map/ppermute | solution.py:216
  211.8 48.9 %collective-permute-start.17 = (f32[2,2,12,768]{3,2,1,0:T(8,128)S(1)}, f32[2,2,12,768]{3,2,1,0:T(8,128)S(1)}, u32[]{:S(2)}, u32[]{:S(2)}) collective-permute-start(f32[2,2,12,768]{3,2,1,0:T(8,128)S(1)} %maximum_select_fusion.8), channel_id=1, source_target_pairs={{0,64},{1,65},{2,66},{3,67},{4,68},{5,69},{6,70},{7,71},{8,72},{9,... | collective-permute-start | bytes 442376 | tf_op jit(solution)/shard_map/ppermute | solution.py:216
  214.2 46.5 %collective-permute-start.18 = (f32[2,2,12,768]{3,2,1,0:T(8,128)S(1)}, f32[2,2,12,768]{3,2,1,0:T(8,128)S(1)}, u32[]{:S(2)}, u32[]{:S(2)}) collective-permute-start(f32[2,2,12,768]{3,2,1,0:T(8,128)S(1)} %maximum_select_fusion.8), channel_id=1, source_target_pairs={{0,96},{1,97},{2,98},{3,99},{4,100},{5,101},{6,102},{7,103},{8,104... | collective-permute-start | bytes 442376 | tf_op jit(solution)/shard_map/ppermute | solution.py:216
  215.4 37.5 %collective-permute-start.10 = (bf16[160,512]{1,0:T(8,128)(2,1)S(1)}, bf16[160,512]{1,0:T(8,128)(2,1)S(1)}, u32[]{:S(2)}, u32[]{:S(2)}) collective-permute-start(bf16[160,512]{1,0:T(8,128)(2,1)S(1)} %add_convert_fusion), channel_id=1, source_target_pairs={{0,1},{1,0},{2,3},{3,2},{4,5},{5,4},{6,7},{7,6},{8,9},{9,8},{10,11... | collective-permute-start | bytes 491528 | tf_op jit(solution)/shard_map/ppermute | solution.py:216
  217.8 35.1 %collective-permute-start.11 = (bf16[160,512]{1,0:T(8,128)(2,1)S(1)}, bf16[160,512]{1,0:T(8,128)(2,1)S(1)}, u32[]{:S(2)}, u32[]{:S(2)}) collective-permute-start(bf16[160,512]{1,0:T(8,128)(2,1)S(1)} %add_convert_fusion), channel_id=1, source_target_pairs={{0,2},{1,3},{2,0},{3,1},{4,6},{5,7},{6,4},{7,5},{8,10},{9,11},{10,... | collective-permute-start | bytes 491528 | tf_op jit(solution)/shard_map/ppermute | solution.py:216
  250.1 5.4 %collective-permute-start.12 = (bf16[160,512]{1,0:T(8,128)(2,1)S(1)}, bf16[160,512]{1,0:T(8,128)(2,1)S(1)}, u32[]{:S(2)}, u32[]{:S(2)}) collective-permute-start(bf16[160,512]{1,0:T(8,128)(2,1)S(1)} %add_convert_fusion), channel_id=1, source_target_pairs={{0,3},{1,2},{2,1},{3,0},{4,7},{5,6},{6,5},{7,4},{8,11},{9,10},{10,... | collective-permute-start | bytes 491528 | tf_op jit(solution)/shard_map/ppermute | solution.py:216
  256.6 10.5 %collective-permute-start.13 = (bf16[4,160,512]{2,1,0:T(8,128)(2,1)}, bf16[4,160,512]{2,1,0:T(8,128)(2,1)}, u32[]{:S(2)}, u32[]{:S(2)}) collective-permute-start(bf16[4,160,512]{2,1,0:T(8,128)(2,1)} %bitcast.19), channel_id=1, source_target_pairs={{0,8},{1,9},{2,10},{3,11},{4,12},{5,13},{6,14},{7,15},{8,0},{9,1},... | collective-permute-start | bytes 1966088 | tf_op jit(solution)/shard_map/ppermute | solution.py:216
  271.9 20.9 %copy-start.1 = (f32[192,512]{1,0:T(8,128)S(1)}, f32[192,512]{1,0:T(8,128)}, u32[]{:S(2)}) copy-start(f32[192,512]{1,0:T(8,128)} %param.16) | copy-start | bytes 1179652
  280.1 1.6 copy-start.2

commit v2 on v1

v2 whole, which is shorter than its diff:
```python
import math

import jax
import jax.numpy as jnp
from jax import lax
from jax.experimental import pallas as pl
from jax.experimental.pallas import tpu as pltpu
from jax.sharding import PartitionSpec as P

P1 = 256
P2 = 512
C = 1536
N_SEQ = 16
N_CH = 8
N_CHIP = N_SEQ // 2
WIDTH = C // N_CH
OWNED = WIDTH // N_SEQ
ROWS = P1 // N_SEQ
LENGTH = ROWS * P2
LANES = P2 // 128
HEIGHT = LANES * ROWS
BLOCK = 96
STEPS = WIDTH // BLOCK
PIECES = 8
FINAL_BLOCK = 48
FORWARD_GROUP = 6
BACKWARD_GROUP = 3
SUM_ROWS = 2 * OWNED
HIGH_ONE = P2 // PIECES
HIGH_TWO = P1 // PIECES
PIECE_ROWS = 2 * HIGH_ONE + HIGH_TWO
AXES = ("seq", "ch")
MESSAGE_ORDER = (0, 2, 6, 3, 7, 1, 4, 5)

flt = jnp.float32
half = jnp.bfloat16


def params():
    return pltpu.CompilerParams(vmem_limit_bytes=63 * 1024 * 1024)


def cost(flops, moved):
    return pl.CostEstimate(flops=int(flops), bytes_accessed=int(moved), transcendentals=0)


def nn(a, b):
    return lax.dot_general(a, b, (((1,), (0,)), ((), ())), preferred_element_type=flt)


def nt(a, b):
    return lax.dot_general(a, b, (((1,), (1,)), ((), ())), preferred_element_type=flt)


def tn(a, b):
    return lax.dot_general(a, b, (((0,), (0,)), ((), ())), preferred_element_type=flt)


def to_slabs(mat, out_ref, index=()):
    for l in range(LANES):
        slab = mat[..., l * 128 : (l + 1) * 128]
        out_ref[(slice(None), *index, slice(l * ROWS, (l + 1) * ROWS))] = slab


def from_slabs(ref, index=()):
    slabs = [
        ref[(slice(None), *index, slice(l * ROWS, (l + 1) * ROWS))] for l in range(LANES)
    ]
    return jnp.concatenate(slabs, axis=-1)


def split_kernel(x_ref, out_ref):
    to_slabs(x_ref[...].reshape(BLOCK, ROWS, P2), out_ref)


def gate_kernel(g_ref, z_ref, keep_ref, send_ref):
    prod = (g_ref[...].astype(flt) * z_ref[...].astype(flt)).astype(half)
    mats = prod.reshape(BLOCK // (2 * OWNED), 2, OWNED, ROWS, P2)
    core = lax.axis_index("seq") % 2

    @pl.when(core == 0)
    def _():
        to_slabs(mats[:, 0], keep_ref, (slice(None),))
        to_slabs(mats[:, 1], send_ref, (slice(None),))

    @pl.when(core == 1)
    def _():
        to_slabs(mats[:, 1], keep_ref, (slice(None),))
        to_slabs(mats[:, 0], send_ref, (slice(None),))


def join_kernel(x_ref, out_ref):
    out_ref[...] = from_slabs(x_ref).reshape(BLOCK, LENGTH)


def final_kernel(h_ref, g_ref, four_ref, out_ref):
    for b in range(FINAL_BLOCK // 16):
        rows = slice(b * 16, b * 16 + 16)
        prod = nn(from_slabs(h_ref.at[rows]).reshape(16 * ROWS, P2), four_ref[...])
        prod = prod.reshape(16, LENGTH)
        out_ref[rows, :] = (g_ref[rows, :].astype(flt) * prod).astype(half)


def flat(n):
    return pl.BlockSpec((n, LENGTH), lambda i: (i, 0))


def mats(n):
    return pl.BlockSpec((n, HEIGHT, 128), lambda i: (i, 0, 0))


FLAT_SHAPE = jax.ShapeDtypeStruct((WIDTH, LENGTH), half)
MATS_SHAPE = jax.ShapeDtypeStruct((WIDTH, HEIGHT, 128), half)
SIZE = WIDTH * LENGTH * 2


def split(x):
    return pl.pallas_call(
        split_kernel, grid=(STEPS,), in_specs=[flat(BLOCK)], out_specs=mats(BLOCK), out_shape=MATS_SHAPE,
        compiler_params=params(), cost_estimate=cost(0, 2 * SIZE), name="split_rows",
    )(x)


def gate(g, z):
    spec = pl.BlockSpec((BLOCK // (2 * OWNED), OWNED, HEIGHT, 128), lambda i: (i, 0, 0, 0))
    shape = jax.ShapeDtypeStruct((N_CHIP, OWNED, HEIGHT, 128), half)
    return pl.pallas_call(
        gate_kernel, grid=(STEPS,), in_specs=[flat(BLOCK), flat(BLOCK)], out_specs=[spec, spec],
        out_shape=[shape, shape], compiler_params=params(), cost_estimate=cost(0, 3 * SIZE),
        name="gate_rows",
    )(g, z)


def join(x):
    return pl.pallas_call(
        join_kernel, grid=(STEPS,), in_specs=[mats(BLOCK)], out_specs=flat(BLOCK), out_shape=FLAT_SHAPE,
        compiler_params=params(), cost_estimate=cost(0, 2 * SIZE), name="join_rows",
    )(x)


def final(h, g, four):
    return pl.pallas_call(
        final_kernel, grid=(WIDTH // FINAL_BLOCK,),
        in_specs=[mats(FINAL_BLOCK), flat(FINAL_BLOCK), pl.BlockSpec((P2, P2), lambda i: (0, 0))],
        out_specs=flat(FINAL_BLOCK), out_shape=FLAT_SHAPE, compiler_params=params(),
        cost_estimate=cost(2 * WIDTH * LENGTH * P2, 3 * SIZE), name="final_rows",
    )(h, g, four)


def forward_kernel(x_ref, one_ref, two_ref, three_ref, kc_ref, kr_ref, h_ref):
    for q in range(FORWARD_GROUP):
        x = from_slabs(x_ref, (q,)).reshape(P1, P2)
        first = (nn(x, one_ref[...]) * kc_ref[q]).astype(half)
        left = (nn(two_ref[...], first) * kr_ref[q]).astype(half)
        second = nn(three_ref[...], left).astype(half)
        to_slabs(second.reshape(N_SEQ, ROWS, P2), h_ref, (q,))


def backward_channels(e_ref, refs, accs, dx_ref, sums_ref):
    x_ref, one_ref, two_ref, three_ref, four_ref, two_t_ref, three_t_ref, kc_ref, kr_ref = refs
    acc_one, acc_two, acc_three, acc_four = accs
    step = pl.program_id(0)
    for q in range(BACKWARD_GROUP):
        kc = kc_ref[q]
        kr = kr_ref[q]
        x = from_slabs(x_ref, (q,)).reshape(P1, P2)
        e = from_slabs(e_ref, (q,)).reshape(P1, P2)
        first_prod = nn(x, one_ref[...])
        first = (first_prod * kc).astype(half)
        left_prod = nn(two_ref[...], first)
        left = (left_prod * kr).astype(half)
        second = nn(three_ref[...], left).astype(half)
        d_second = nt(e, four_ref[...]).astype(half)
        d_left = nn(three_t_ref[...], d_second)
        row_terms = d_left * left_prod
        row_terms = sum(row_terms[:, l * 128 : (l + 1) * 128] for l in range(LANES))
        row_sums = jnp.sum(row_terms.T, axis=0, keepdims=True)
        d_prod = (d_left * kr).astype(half)
        d_first = nn(two_t_ref[...], d_prod).astype(half).astype(flt)
        col_sums = jnp.sum(d_first * first_prod, axis=0, keepdims=True)
        d_inner = (d_first * kc).astype(half)
        d_x = nt(d_inner, one_ref[...]).astype(half)
        to_slabs(d_x.reshape(N_SEQ, ROWS, P2), dx_ref, (q,))
        channel = step * BACKWARD_GROUP + q
        sums_ref[pl.ds(channel, 1), :] = col_sums
        sums_ref[pl.ds(OWNED + channel, 1), 0:P1] = row_sums
        acc_four[...] += tn(second, e)
        acc_three[...] += nt(d_second, left)
        acc_two[...] += nt(d_prod, first)
        acc_one[...] += tn(x, d_inner)


def backward_kernel(*refs):
    e_parts = refs[9 : 9 + N_CHIP]
    dx_ref, sums_ref, keep_ref, send_ref, *accs, e_ref = refs[9 + N_CHIP :]
    step = pl.program_id(0)
    seq = lax.axis_index("seq")
    for offset, ref in zip(MESSAGE_ORDER, e_parts):
        source = seq ^ (2 * offset)
        e_ref[source] = ref[0]
        e_ref[source ^ 1] = ref[1]

    @pl.when(step == 0)
    def _():
        for ref in (*accs, sums_ref):
            ref[...] = jnp.zeros_like(ref)

    backward_channels(e_ref, refs[:9], accs, dx_ref, sums_ref)
    core = seq % 2
    acc_one, acc_two, acc_three, acc_four = accs

    def write(out_ref, first_piece):
        for p in range(PIECES // 2):
            at = first_piece + p
            wide = slice(at * HIGH_ONE, (at + 1) * HIGH_ONE)
            tall = slice(at * HIGH_TWO, (at + 1) * HIGH_TWO)
            middle = slice(HIGH_ONE, HIGH_ONE + HIGH_TWO)
            dtype = out_ref.dtype
            out_ref[p, 0:HIGH_ONE, :] = acc_one[wide, :].astype(dtype)
            out_ref[p, middle, 0:P1] = acc_two[tall, :].astype(dtype)
            out_ref[p, middle, P1 : 2 * P1] = acc_three[tall, :].astype(dtype)
            out_ref[p, HIGH_ONE + HIGH_TWO : PIECE_ROWS, :] = acc_four[wide, :].astype(dtype)

    for c in range(2):

        @pl.when((step == OWNED // BACKWARD_GROUP - 1) & (core == c))
        def _(c=c):
            write(keep_ref, c * (PIECES // 2))
            write(send_ref, (1 - c) * (PIECES // 2))


def whole(*shape):
    return pl.BlockSpec(shape, lambda q: (0,) * len(shape))


def own(n):
    return pl.BlockSpec((N_SEQ, n, HEIGHT, 128), lambda q: (0, q, 0, 0))


def col(n):
    return pl.BlockSpec((n, 1, P2), lambda q: (q, 0, 0))


def row(n):
    return pl.BlockSpec((n, P1, 1), lambda q: (q, 0, 0))


OWN_SHAPE = jax.ShapeDtypeStruct((N_SEQ, OWNED, HEIGHT, 128), half)
BIG = 2 * P1 * P2 * P2 * OWNED
SMALL = 2 * P1 * P1 * P2 * OWNED


def forward(x, one, two, three, kc, kr):
    n = FORWARD_GROUP
    return pl.pallas_call(
        forward_kernel, grid=(OWNED // n,),
        in_specs=[own(n), whole(P2, P2), whole(P1, P1), whole(P1, P1), col(n), row(n)],
        out_specs=own(n), out_shape=OWN_SHAPE, compiler_params=params(),
        cost_estimate=cost(BIG + 2 * SMALL, 2 * SIZE), name="forward_owned",
    )(x, one, two, three, kc, kr)


ACC_SHAPES = [(P2, P2), (P1, P1), (P1, P1), (P2, P2)]


def backward(args, e_parts):
    n = BACKWARD_GROUP
    piece = (PIECES // 2, PIECE_ROWS, P2)
    return pl.pallas_call(
        backward_kernel, grid=(OWNED // n,),
        in_specs=[
            own(n), whole(P2, P2), whole(P1, P1), whole(P1, P1), whole(P2, P2),
            whole(P1, P1), whole(P1, P1), col(n), row(n),
        ]
        + [pl.BlockSpec((2, n, HEIGHT, 128), lambda q: (0, q, 0, 0))] * N_CHIP,
        out_specs=[own(n), whole(SUM_ROWS, P2), whole(*piece), whole(*piece)],
        out_shape=[
            OWN_SHAPE, jax.ShapeDtypeStruct((SUM_ROWS, P2), flt),
            jax.ShapeDtypeStruct(piece, flt), jax.ShapeDtypeStruct(piece, half),
        ],
        scratch_shapes=[
            *(pltpu.VMEM(s, flt) for s in ACC_SHAPES),
            pltpu.VMEM((N_SEQ, n, HEIGHT, 128), half),
        ],
        compiler_params=params(),
        cost_estimate=cost(5 * BIG + 6 * SMALL, 3 * SIZE), name="backward_owned",
    )(*args, *e_parts)


def swap_pairs(x=0, zh=0, core=0, zl=0, y=0):
    flip_seq = x * 4 + zh * 2 + core
    flip_ch = zl * 4 + y
    return [
        (s * N_CH + c, (s ^ flip_seq) * N_CH + (c ^ flip_ch))
        for s in range(N_SEQ)
        for c in range(N_CH)
    ]


def swap(v, **flips):
    return lax.ppermute(v, AXES, swap_pairs(**flips))


def pick(v, index):
    return lax.dynamic_index_in_dim(v, index, 0, keepdims=False)


def in_order(bit, mine, theirs):
    return jnp.where(bit == 0, jnp.stack([mine, theirs]), jnp.stack([theirs, mine]))


def four_in_order(place, own, near, far, other):
    low = in_order(place & 1, own, near)
    high = in_order(place & 1, far, other)
    return in_order(place >> 1, low, high).reshape(4, *own.shape)


def sum_over_four(v, axes, extra, extra_axes):
    v = v.astype(half)
    got = []
    held = []
    for flips in axes:
        if flips in extra_axes:
            both = swap(jnp.concatenate([v, extra]), **flips)
            got.append(both[:PIECE_ROWS])
            held.append(both[PIECE_ROWS:])
        else:
            got.append(swap(v, **flips))
    one, two, three = got
    return (v.astype(flt) + one.astype(flt)) + (two.astype(flt) + three.astype(flt)), held


def reduce_grads(keep, send, y):
    kept = keep + swap(send, core=1).astype(flt)
    got = [swap(pick(kept, y ^ d).astype(half), y=d).astype(flt) for d in (1, 2, 3)]
    return pick(kept, y) + got[0] + got[1] + got[2]


def gather_grads(mine, core, y):
    near, far, other = (swap(mine, y=d) for d in (1, 2, 3))
    mine = four_in_order(y, mine, near, far, other)
    both = in_order(core, mine, swap(mine, core=1))
    return both.reshape(PIECES, PIECE_ROWS, P2)


def after(*values):
    return lax.optimization_barrier(values)


def exchange(v):
    rows = v.reshape(-1, 128)
    return lax.all_to_all(rows, "seq", split_axis=0, concat_axis=0, tiled=True)


def exchange_by_chip(keep, send, chip):
    sibling = swap(send, core=1)
    parts = []
    for offset in MESSAGE_ORDER:
        message = jnp.stack([pick(keep, chip ^ offset), pick(sibling, chip ^ offset)])
        if offset:
            message = swap(message, x=offset >> 1, zh=offset & 1)
        parts.append(message)
    return parts


def local(
    inputs,
    gating,
    upstream,
    factor_one,
    factor_two,
    factor_three,
    factor_four,
    kernel_cols,
    kernel_rows,
):
    seq = lax.axis_index("seq")
    ch = lax.axis_index("ch")
    x_at, zh_at, core_at, y_at = seq >> 2, (seq >> 1) & 1, seq & 1, ch & 3
    owned = (N_SEQ, OWNED, HEIGHT, 128)
    by_channel = (WIDTH, HEIGHT, 128)
    kc = lax.dynamic_slice_in_dim(kernel_cols, seq * OWNED, OWNED, 0).reshape(OWNED, 1, P2)
    kr = lax.dynamic_slice_in_dim(kernel_rows, seq * OWNED, OWNED, 0).reshape(OWNED, P1, 1)

    x_own = exchange(split(inputs)).reshape(owned)
    e_parts = exchange_by_chip(*gate(upstream, gating), seq >> 1)
    h_own = forward(x_own, factor_one, factor_two, factor_three, kc, kr)
    h_own, *e_parts = after(h_own, *e_parts)
    h_rows = exchange(h_own).reshape(by_channel)
    args = (
        x_own, factor_one, factor_two, factor_three, factor_four, factor_two.T, factor_three.T,
        kc, kr,
    )
    dx_own, sums, keep, send = backward(args, e_parts)
    sums = sums.astype(half)
    sums = in_order(core_at, sums, swap(sums, core=1)).reshape(2 * SUM_ROWS, P2)
    mine = reduce_grads(keep, send, y_at)
    mine, sums, h_rows = after(mine, sums, h_rows)
    over_x = [dict(x=1), dict(x=2), dict(x=3)]
    mine, held = sum_over_four(mine, over_x, sums, over_x)
    sums = four_in_order(x_at, sums, *held).reshape(8 * SUM_ROWS, P2)
    over_z = [dict(zl=1), dict(zh=1), dict(zh=1, zl=1)]
    mine, held = sum_over_four(mine, over_z, sums, over_z[1:2])
    sums = in_order(zh_at, sums, held[0]).reshape(2, 4, 2, SUM_ROWS, P2)
    mine, sums, dx_own = after(mine.astype(half), sums, dx_own)
    dx_rows = exchange(dx_own).reshape(by_channel)
    sums = sums.swapaxes(0, 1).reshape(N_SEQ, SUM_ROWS, P2).astype(flt)
    cols = sums[:, 0:OWNED].reshape(WIDTH, P2)
    rows = sums[:, OWNED : 2 * OWNED, 0:P1].reshape(WIDTH, P1)
    total = gather_grads(mine, core_at, y_at)
    gating_grad = final(h_rows, upstream, factor_four)
    total = total.astype(flt)
    scale_one = 1.0 / math.sqrt(P1 * C)
    scale_two = 1.0 / math.sqrt(P2 * C)
    one_grad = total[:, 0:HIGH_ONE, :].reshape(P2, P2) * scale_one
    mid = total[:, HIGH_ONE : HIGH_ONE + HIGH_TWO, :].reshape(P1, P2) * scale_two
    four_grad = total[:, HIGH_ONE + HIGH_TWO : PIECE_ROWS, :].reshape(P2, P2) * scale_one
    small = (
        gating_grad,
        one_grad,
        mid[:, 0:P1],
        mid[:, P1 : 2 * P1],
        four_grad,
        cols * (1.0 / math.sqrt(P1)),
        rows * (1.0 / math.sqrt(P2)),
    )
    dx_rows, *small = after(dx_rows, *small)
    return join(dx_rows), *small


def solution(mesh):
    in_specs = (
        P("ch", "seq"),
        P("ch", "seq"),
        P("ch", "seq"),
        P(),
        P(),
        P(),
        P(),
        P("ch", None),
        P("ch", None),
    )
    out_specs = (P("ch", "seq"), P("ch", "seq"), P(), P(), P(), P(), P("ch", None), P("ch", None))
    return jax.shard_map(local, mesh=mesh, in_specs=in_specs, out_specs=out_specs, check_vma=False)
```

time: 297 us -> 224 us (0.75)
  waiting for transfers between devices: 117 us -> 89.4 us
  Pallas kernels: 78.5 us -> 55.5 us
  local copies, waits for them, and re-layouts: 16.5 us -> 8.09 us
  starting transfers between devices: 61.9 us -> 55.4 us
  other arithmetic: 18.3 us -> 12 us
    all_to_all x4 -> x3, waiting for transfers between devices: 64.3 us -> 10 us  [exchange(): return lax.all_to_all(rows, 'seq', split_axis=0, concat_axis=0, tiled=True)]
    ppermute x19 -> x23, waiting for transfers between devices: 52.6 us -> 79.4 us  [swap(): return lax.ppermute(v, AXES, swap_pairs(**flips))]
    pallas_call x6, Pallas kernels: 78.5 us -> 55.5 us  [the longest x1 25.7 us: backward(): pl.pallas_call(backward_kernel, grid=(OWNED // n,), in_specs=[own(n), who...]
    all_to_all x4 -> x3, starting transfers between devices: 33.3 us -> 21.2 us  [exchange(): return lax.all_to_all(rows, 'seq', split_axis=0, concat_axis=0, tiled=True)]
    unnamed x17 -> x18, local copies, waits for them, and re-layouts: 8.31 us -> 2.23 us
    ppermute x19 -> x23, starting transfers between devices: 28.6 us -> 34.2 us  [swap(): return lax.ppermute(v, AXES, swap_pairs(**flips))]
    another operation x0 -> x8, other arithmetic: none -> 4.08 us  [exchange_by_chip(): jnp.stack([pick(keep, chip ^ offset), pick(sibling, chip ^ offset)])]
    div x2 -> x0, other arithmetic: 3.39 us -> none  [the longest x1 1.77 us: local(): sums[:, 0:P2] / math.sqrt(P1)]
  transfers between devices with their start and end apart: 23 -> 26, of which waited for: 7 -> 17; matrix products, arithmetic and copies ran while one was open for 10% -> 9% of each run, Pallas kernels for 10% -> 22%
where the time goes in v2:
time: 224 us; the launch traced here: 221 us
  waiting for transfers between devices  89.4 us (40%)
  Pallas kernels  55.5 us (25%)
  starting transfers between devices  55.4 us (25%)
  other arithmetic  12 us (5%)
  local copies, waits for them, and re-layouts  8.09 us (4%)
    ppermute x23, waiting for transfers between devices, swap(): return lax.ppermute(v, AXES, swap_pairs(**flips))  79.4 us
    ppermute x23, starting transfers between devices, swap(): return lax.ppermute(v, AXES, swap_pairs(**flips))  34.2 us
    pallas_call x1, Pallas kernels, backward(): pl.pallas_call(backward_kernel, grid=(OWNED // n,), in_specs=[own(n), who...  25.7 us
    all_to_all x3, starting transfers between devices, exchange(): return lax.all_to_all(rows, 'seq', split_axis=0, concat_axis=0, tiled=True)  21.2 us
    all_to_all x3, waiting for transfers between devices, exchange(): return lax.all_to_all(rows, 'seq', split_axis=0, concat_axis=0, tiled=True)  10 us
    pallas_call x1, Pallas kernels, forward(): pl.pallas_call(forward_kernel, grid=(OWNED // n,), in_specs=[own(n), whol...  9.78 us
    pallas_call x1, Pallas kernels, final(): pl.pallas_call(final_kernel, grid=(WIDTH // FINAL_BLOCK,), in_specs=[mats...  7.02 us
    pallas_call x1, Pallas kernels, gate(): pl.pallas_call(gate_kernel, grid=(STEPS,), in_specs=[flat(BLOCK), flat(BL...  5.75 us
  transfers between devices with their start and end apart: 26, of which 17 were waited for; matrix products, arithmetic and copies ran while one was open for 9% of the time, Pallas kernels for 22%

profile of v2, /device:TPU:1, one launch (start us, length us, event | category | flops | bytes accessed | tf_op | source)
XLA Modules:
  0.0 221.3 jit_solution(17787038696568728856)
XLA Ops:
  0.6 3.6 %split_rows.1 = bf16[192,64,128]{2,1,0:T(8,128)(2,1)} custom-call(bf16[192,8192]{1,0:T(8,128)(2,1)} %x_ref.1), custom_call_target="tpu_custom_call" | custom-call | bytes 6291456 | tf_op jit(solution)/shard_map/split_rows/pallas_call | solution.py:118
  4.3 9.1 %all-to-all-start = ((bf16[16,768,128]{2,1,0:T(8,128)(2,1)}), bf16[16,768,128]{2,1,0:T(8,128)(2,1)}, u32[]{:S(2)}, u32[]{:S(2)}) async-start(bf16[16,768,128]{2,1,0:T(8,128)(2,1)} %bitcast.56), calls=%async_computation | async-start | bytes 6291456 | tf_op jit(solution)/shard_map/all_to_all | solution.py:352
  13.4 5.8 %gate_rows.1 = (bf16[8,12,64,128]{3,2,1,0:T(8,128)(2,1)}, bf16[8,12,64,128]{3,2,1,0:T(8,128)(2,1)}) custom-call(bf16[192,8192]{1,0:T(8,128)(2,1)} %g_ref.3, bf16[192,8192]{1,0:T(8,128)(2,1)} %z_ref.1), custom_call_target="tpu_custom_call" | custom-call | bytes 9437184 | tf_op jit(solution)/shard_map/gate_rows/pallas_call | solution.py:127
  24.6 1.9 collective-permute-start.2
  26.5 2.8 %collective-permute-start.3 = (bf16[2,12,64,128]{3,2,1,0:T(8,128)(2,1)S(1)}, bf16[2,12,64,128]{3,2,1,0:T(8,128)(2,1)}, u32[]{:S(2)}, u32[]{:S(2)}) collective-permute-start(bf16[2,12,64,128]{3,2,1,0:T(8,128)(2,1)S(1)} %pad_maximum_fusion.3), channel_id=1, source_target_pairs={{0,48},{1,49},{2,50},{3,51},{4,52},{5,53},{6,54},{7,55},{8,56},{9,... | collective-permute-start | bytes 1179656 | tf_op jit(solution)/shard_map/ppermute | solution.py:301
  31.5 2.7 %collective-permute-start.5 = (bf16[2,12,64,128]{3,2,1,0:T(8,128)(2,1)}, bf16[2,12,64,128]{3,2,1,0:T(8,128)(2,1)}, u32[]{:S(2)}, u32[]{:S(2)}) collective-permute-start(bf16[2,12,64,128]{3,2,1,0:T(8,128)(2,1)} %pad_maximum_fusion.5), channel_id=1, source_target_pairs={{0,16},{1,17},{2,18},{3,19},{4,20},{5,21},{6,22},{7,23},{8,24},{9,... | collective-permute-start | bytes 1179656 | tf_op jit(solution)/shard_map/ppermute | solution.py:301
  35.8 23.4 %collective-permute-done.1.refs_10_ = bf16[2,12,64,128]{3,2,1,0:T(8,128)(2,1)S(1)} collective-permute-done((bf16[2,12,64,128]{3,2,1,0:T(8,128)(2,1)S(1)}, bf16[2,12,64,128]{3,2,1,0:T(8,128)(2,1)S(1)}, u32[]{:S(2)}, u32[]{:S(2)}) %collective-permute-start.1) | collective-permute-done | bytes 393248 | tf_op jit(solution)/shard_map/ppermute | solution.py:301
  59.1 7.8 %collective-permute-start.6 = (bf16[2,12,64,128]{3,2,1,0:T(8,128)(2,1)}, bf16[2,12,64,128]{3,2,1,0:T(8,128)(2,1)}, u32[]{:S(2)}, u32[]{:S(2)}) collective-permute-start(bf16[2,12,64,128]{3,2,1,0:T(8,128)(2,1)} %pad_maximum_fusion.6), channel_id=1, source_target_pairs={{0,64},{1,65},{2,66},{3,67},{4,68},{5,69},{6,70},{7,71},{8,72},{9,... | collective-permute-start | bytes 1179656 | tf_op jit(solution)/shard_map/ppermute | solution.py:301
  68.5 9.8 %forward_owned.1 = bf16[16,12,64,128]{3,2,1,0:T(8,128)(2,1)} custom-call(bf16[16,12,64,128]{3,2,1,0:T(8,128)(2,1)} %bitcast.1.x_ref.refs_0_, bf16[512,512]{1,0:T(8,128)(2,1)} %refs_1_.1, bf16[256,256]{1,0:T(8,128)(2,1)} %refs_2_.1, bf16[256,256]{1,0:T(8,128)(2,1)} %refs_3_.1, f32[12,1,512]{2,1,0:T(1,128)} %reshape.372.kc_ref.refs_7_, ...), custom_call_target="tpu_custom_call" | custom-call | flops 3221225472 | bytes 6291456 | tf_op jit(solution)/shard_map/forward_owned/pallas_call | solution.py:255
  78.3 7.7 %collective-permute-done.6.refs_15_ = bf16[2,12,64,128]{3,2,1,0:T(8,128)(2,1)} collective-permute-done((bf16[2,12,64,128]{3,2,1,0:T(8,128)(2,1)}, bf16[2,12,64,128]{3,2,1,0:T(8,128)(2,1)}, u32[]{:S(2)}, u32[]{:S(2)}) %collective-permute-start.6) | collective-permute-done | bytes 393248 | tf_op jit(solution)/shard_map/ppermute | solution.py:301
  86.0 9.2 %collective-permute-done.7.refs_16_ = bf16[2,12,64,128]{3,2,1,0:T(8,128)(2,1)} collective-permute-done((bf16[2,12,64,128]{3,2,1,0:T(8,128)(2,1)}, bf16[2,12,64,128]{3,2,1,0:T(8,128)(2,1)}, u32[]{:S(2)}, u32[]{:S(2)}) %collective-permute-start.7) | collective-permute-done | bytes 393248 | tf_op jit(solution)/shard_map/ppermute | solution.py:301
  95.2 5.2 %all-to-all-start.1 = ((bf16[16,768,128]{2,1,0:T(8,128)(2,1)}), bf16[16,768,128]{2,1,0:T(8,128)(2,1)}, u32[]{:S(2)}, u32[]{:S(2)}) async-start(bf16[16,768,128]{2,1,0:T(8,128)(2,1)} %bitcast.57), calls=%async_computation.1 | async-start | bytes 6291456 | tf_op jit(solution)/shard_map/all_to_all | solution.py:352
  102.0 25.7 %backward_owned.1 = (bf16[16,12,64,128]{3,2,1,0:T(8,128)(2,1)}, f32[24,512]{1,0:T(8,128)}, f32[4,160,512]{2,1,0:T(8,128)}, bf16[4,160,512]{2,1,0:T(8,128)(2,1)}) custom-call(bf16[16,12,64,128]{3,2,1,0:T(8,128)(2,1)} %bitcast.1.x_ref.refs_0_, bf16[512,512]{1,0:T(8,128)(2,1)} %refs_1_.1, bf16[256,256]{1,0:T(8,128)(2,1)} %refs_2_.1, bf16[256,256]{1,0:T(8,128)(2,1)} %refs_3_.1, ...), custom_call_target="tpu_custom_call" | custom-call | flops 12884901888 | bytes 9437184 | tf_op jit(solution)/shard_map/backward_owned/pallas_call | solution.py:269
  131.8 3.0 %collective-permute-start.10 = (bf16[160,512]{1,0:T(8,128)(2,1)S(1)}, bf16[160,512]{1,0:T(8,128)(2,1)S(1)}, u32[]{:S(2)}, u32[]{:S(2)}) collective-permute-start(bf16[160,512]{1,0:T(8,128)(2,1)S(1)} %get-tuple-element.86), channel_id=1, source_target_pairs={{0,2},{1,3},{2,0},{3,1},{4,6},{5,7},{6,4},{7,5},{8,10},{9,11},{10,... | collective-permute-start | bytes 491528 | tf_op jit(solution)/shard_map/ppermute | solution.py:301
  135.6 3.3 %collective-permute-done.10 = bf16[160,512]{1,0:T(8,128)(2,1)S(1)} collective-permute-done((bf16[160,512]{1,0:T(8,128)(2,1)S(1)}, bf16[160,512]{1,0:T(8,128)(2,1)S(1)}, u32[]{:S(2)}, u32[]{:S(2)}) %collective-permute-start.10) | collective-permute-done | bytes 163872 | tf_op jit(solution)/shard_map/ppermute | solution.py:301
  138.9 4.0 %collective-permute-done.11 = bf16[160,512]{1,0:T(8,128)(2,1)S(1)} collective-permute-done((bf16[160,512]{1,0:T(8,128)(2,1)S(1)}, bf16[160,512]{1,0:T(8,128)(2,1)S(1)}, u32[]{:S(2)}, u32[]{:S(2)}) %collective-permute-start.11) | collective-permute-done | bytes 163872 | tf_op jit(solution)/shard_map/ppermute | solution.py:301
  144.4 1.8 collective-permute-start.15
  146.9 1.9 collective-permute-done.13
  148.8 2.2 %collective-permute-done.15 = bf16[208,512]{1,0:T(8,128)(2,1)S(1)} collective-permute-done((bf16[208,512]{1,0:T(8,128)(2,1)S(1)}, bf16[208,512]{1,0:T(8,128)(2,1)S(1)}, u32[]{:S(2)}, u32[]{:S(2)}) %collective-permute-start.15) | collective-permute-done | bytes 213024 | tf_op jit(solution)/shard_map/ppermute | solution.py:301
  151.1 4.8 %collective-permute-done.14 = bf16[208,512]{1,0:T(8,128)(2,1)S(1)} collective-permute-done((bf16[208,512]{1,0:T(8,128)(2,1)S(1)}, bf16[208,512]{1,0:T(8,128)(2,1)S(1)}, u32[]{:S(2)}, u32[]{:S(2)}) %collective-permute-start.14) | collective-permute-done | bytes 213024 | tf_op jit(solution)/shard_map/ppermute | solution.py:301
  156.0 2.7 %collective-permute-start.17 = (bf16[352,512]{1,0:T(8,128)(2,1)S(1)}, bf16[352,512]{1,0:T(8,128)(2,1)S(1)}, u32[]{:S(2)}, u32[]{:S(2)}) collective-permute-start(bf16[352,512]{1,0:T(8,128)(2,1)S(1)} %pad_maximum_fusion.8), channel_id=1, source_target_pairs={{0,16},{1,17},{2,18},{3,19},{4,20},{5,21},{6,22},{7,23},{8,24},{9,... | collective-permute-start | bytes 1081352 | tf_op jit(solution)/shard_map/ppermute | solution.py:301
  159.5 6.0 %collective-permute-done.17 = bf16[352,512]{1,0:T(8,128)(2,1)S(1)} collective-permute-done((bf16[352,512]{1,0:T(8,128)(2,1)S(1)}, bf16[352,512]{1,0:T(8,128)(2,1)S(1)}, u32[]{:S(2)}, u32[]{:S(2)}) %collective-permute-start.17) | collective-permute-done | bytes 360480 | tf_op jit(solution)/shard_map/ppermute | solution.py:301
  165.6 3.8 %collective-permute-done.16 = bf16[160,512]{1,0:T(8,128)(2,1)S(1)} collective-permute-done((bf16[160,512]{1,0:T(8,128)(2,1)S(1)}, bf16[160,512]{1,0:T(8,128)(2,1)S(1)}, u32[]{:S(2)}, u32[]{:S(2)}) %collective-permute-start.16) | collective-permute-done | bytes 163872 | tf_op jit(solution)/shard_map/ppermute | solution.py:301
  171.0 6.8 %all-to-all-start.2 = ((bf16[16,768,128]{2,1,0:T(8,128)(2,1)}), bf16[16,768,128]{2,1,0:T(8,128)(2,1)}, u32[]{:S(2)}, u32[]{:S(2)}) async-start(bf16[16,768,128]{2,1,0:T(8,128)(2,1)} %bitcast.25), calls=%async_computation.2 | async-start | bytes 6291456 | tf_op jit(solution)/shard_map/all_to_all | solution.py:352
  179.1 2.6 %collective-permute-start.20 = (bf16[160,512]{1,0:T(8,128)(2,1)S(1)}, bf16[160,512]{1,0:T(8,128)(2,1)S(1)}, u32[]{:S(2)}, u32[]{:S(2)}) collective-permute-start(bf16[160,512]{1,0:T(8,128)(2,1)S(1)} %add_convert_fusion), channel_id=1, source_target_pairs={{0,2},{1,3},{2,0},{3,1},{4,6},{5,7},{6,4},{7,5},{8,10},{9,11},{10,... | collective-permute-start | bytes 491528 | tf_op jit(solution)/shard_map/ppermute | solution.py:301
  181.7 1.8 collective-permute-done.19
  183.5 6.0 %collective-permute-done.20 = bf16[160,512]{1,0:T(8,128)(2,1)S(1)} collective-permute-done((bf16[160,512]{1,0:T(8,128)(2,1)S(1)}, bf16[160,512]{1,0:T(8,128)(2,1)S(1)}, u32[]{:S(2)}, u32[]{:S(2)}) %collective-permute-start.20) | collective-permute-done | bytes 163872 | tf_op jit(solution)/shard_map/ppermute | solution.py:301
  189.5 2.5 %collective-permute-done.21 = bf16[160,512]{1,0:T(8,128)(2,1)S(1)} collective-permute-done((bf16[160,512]{1,0:T(8,128)(2,1)S(1)}, bf16[160,512]{1,0:T(8,128)(2,1)S(1)}, u32[]{:S(2)}, u32[]{:S(2)}) %collective-permute-start.21) | collective-permute-done | bytes 163872 | tf_op jit(solution)/shard_map/ppermute | solution.py:301
  194.1 7.0 %final_rows.1 = bf16[192,8192]{1,0:T(8,128)(2,1)} custom-call(bf16[192,64,128]{2,1,0:T(8,128)(2,1)} %bitcast.13.h_ref, bf16[192,8192]{1,0:T(8,128)(2,1)} %g_ref.3, bf16[512,512]{1,0:T(8,128)(2,1)} %four_ref.1), custom_call_target="tpu_custom_call" | custom-call | flops 1610612736 | bytes 9437184 | tf_op jit(solution)/shard_map/final_rows/pallas_call | solution.py:142
  202.7 2.0 maximum_select_fusion
  207.6 10.0 %all-to-all-done.2 = bf16[16,768,128]{2,1,0:T(8,128)(2,1)} async-done(((bf16[16,768,128]{2,1,0:T(8,128)(2,1)}), bf16[16,768,128]{2,1,0:T(8,128)(2,1)}, u32[]{:S(2)}, u32[]{:S(2)}) %all-to-all-start.2) | async-done | bytes 3145760 | tf_op jit(solution)/shard_map/all_to_all | solution.py:352
  217.7 3.6 %join_rows.1 = bf16[192,8192]{1,0:T(8,128)(2,1)} custom-call(bf16[192,64,128]{2,1,0:T(8,128)(2,1)} %bitcast.26.x_ref), custom_call_target="tpu_custom_call" | custom-call | bytes 6291456 | tf_op jit(solution)/shard_map/join_rows/pallas_call | solution.py:135
  (89 shorter events, 29.9 us)
Async XLA Ops:
  0.6 21.2 %copy-start = (f32[192,512]{1,0:T(8,128)S(1)}, f32[192,512]{1,0:T(8,128)}, u32[]{:S(2)}) copy-start(f32[192,512]{1,0:T(8,128)} %param.16) | copy-start | bytes 1179652
  4.3 64.2 %all-to-all-start = ((bf16[16,768,128]{2,1,0:T(8,128)(2,1)}), bf16[16,768,128]{2,1,0:T(8,128)(2,1)}, u32[]{:S(2)}, u32[]{:S(2)}) async-start(bf16[16,768,128]{2,1,0:T(8,128)(2,1)} %bitcast.56), calls=%async_computation | async-start | bytes 6291456 | tf_op jit(solution)/shard_map/all_to_all | solution.py:352
  19.2 3.6 %collective-permute-start = (bf16[8,12,64,128]{3,2,1,0:T(8,128)(2,1)}, bf16[8,12,64,128]{3,2,1,0:T(8,128)(2,1)S(1)}, u32[]{:S(2)}, u32[]{:S(2)}) collective-permute-start(bf16[8,12,64,128]{3,2,1,0:T(8,128)(2,1)} %get-tuple-element.38), channel_id=1, source_target_pairs={{0,8},{1,9},{2,10},{3,11},{4,12},{5,13},{6,14},{7,15},{8,0},{9,1},... | collective-permute-start | bytes 4718600 | tf_op jit(solution)/shard_map/ppermute | solution.py:301
  23.0 36.2 %collective-permute-start.1 = (bf16[2,12,64,128]{3,2,1,0:T(8,128)(2,1)S(1)}, bf16[2,12,64,128]{3,2,1,0:T(8,128)(2,1)S(1)}, u32[]{:S(2)}, u32[]{:S(2)}) collective-permute-start(bf16[2,12,64,128]{3,2,1,0:T(8,128)(2,1)S(1)} %pad_maximum_fusion.1), channel_id=1, source_target_pairs={{0,32},{1,33},{2,34},{3,35},{4,36},{5,37},{6,38},{7,39},{8,40},{9,... | collective-permute-start | bytes 1179656 | tf_op jit(solution)/shard_map/ppermute | solution.py:301
  24.6 42.3 %collective-permute-start.2 = (bf16[2,12,64,128]{3,2,1,0:T(8,128)(2,1)S(1)}, bf16[2,12,64,128]{3,2,1,0:T(8,128)(2,1)S(1)}, u32[]{:S(2)}, u32[]{:S(2)}) collective-permute-start(bf16[2,12,64,128]{3,2,1,0:T(8,128)(2,1)S(1)} %pad_maximum_fusion.2), channel_id=1, source_target_pairs={{0,96},{1,97},{2,98},{3,99},{4,100},{5,101},{6,102},{7,103},{8,104... | collective-permute-start | bytes 1179656 | tf_op jit(solution)/shard_map/ppermute | solution.py:301
  26.5 51.8 %collective-permute-start.3 = (bf16[2,12,64,128]{3,2,1,0:T(8,128)(2,1)S(1)}, bf16[2,12,64,128]{3,2,1,0:T(8,128)(2,1)}, u32[]{:S(2)}, u32[]{:S(2)}) collective-permute-start(bf16[2,12,64,128]{3,2,1,0:T(8,128)(2,1)S(1)} %pad_maximum_fusion.3), channel_id=1, source_target_pairs={{0,48},{1,49},{2,50},{3,51},{4,52},{5,53},{6,54},{7,55},{8,56},{9,... | collective-permute-start | bytes 1179656 | tf_op jit(solution)/shard_map/ppermute | solution.py:301
  30.0 48.2 %collective-permute-start.4 = (bf16[2,12,64,128]{3,2,1,0:T(8,128)(2,1)}, bf16[2,12,64,128]{3,2,1,0:T(8,128)(2,1)}, u32[]{:S(2)}, u32[]{:S(2)}) collective-permute-start(bf16[2,12,64,128]{3,2,1,0:T(8,128)(2,1)} %pad_maximum_fusion.4), channel_id=1, source_target_pairs={{0,112},{1,113},{2,114},{3,115},{4,116},{5,117},{6,118},{7,119},{8... | collective-permute-start | bytes 1179656 | tf_op jit(solution)/shard_map/ppermute | solution.py:301
  31.5 46.8 %collective-permute-start.5 = (bf16[2,12,64,128]{3,2,1,0:T(8,128)(2,1)}, bf16[2,12,64,128]{3,2,1,0:T(8,128)(2,1)}, u32[]{:S(2)}, u32[]{:S(2)}) collective-permute-start(bf16[2,12,64,128]{3,2,1,0:T(8,128)(2,1)} %pad_maximum_fusion.5), channel_id=1, source_target_pairs={{0,16},{1,17},{2,18},{3,19},{4,20},{5,21},{6,22},{7,23},{8,24},{9,... | collective-permute-start | bytes 1179656 | tf_op jit(solution)/shard_map/ppermute | solution.py:301
  59.1 7.8 %copy-start.6 = (bf16[2,12,64,128]{3,2,1,0:T(8,128)(2,1)}, bf16[2,12,64,128]{3,2,1,0:T(8,128)(2,1)S(1)}, u32[]{:S(2)}) copy-start(bf16[2,12,64,128]{3,2,1,0:T(8,128)(2,1)S(1)} %collective-permute-done.1.refs_10_) | copy-start | bytes 1179652
  59.1 26.9 %collective-permute-start.6 = (bf16[2,12,64,128]{3,2,1,0:T(8,128)(2,1)}, bf16[2,12,64,128]{3,2,1,0:T(8,128)(2,1)}, u32[]{:S(2)}, u32[]{:S(2)}) collective-permute-start(bf16[2,12,64,128]{3,2,1,0:T(8,128)(2,1)} %pad_maximum_fusion.6), channel_id=1, source_target_pairs={{0,64},{1,65},{2,66},{3,67},{4,68},{5,69},{6,70},{7,71},{8,72},{9,... | collective-permute-start | bytes 1179656 | tf_op jit(solution)/shard_map/ppermute | solution.py:301
  66.9 28.3 %collective-permute-start.7 = (bf16[2,12,64,128]{3,2,1,0:T(8,128)(2,1)}, bf16[2,12,64,128]{3,2,1,0:T(8,128)(2,1)}, u32[]{:S(2)}, u32[]{:S(2)}) collective-permute-start(bf16[2,12,64,128]{3,2,1,0:T(8,128)(2,1)} %pad_maximum_fusion.7), channel_id=1, source_target_pairs={{0,80},{1,81},{2,82},{3,83},{4,84},{5,85},{6,86},{7,87},{8,88},{9,... | collective-permute-start | bytes 1179656 | tf_op jit(solution)/shard_map/ppermute | solution.py:301
  95.2 5.2 %copy-start.4 = (bf16[256,256]{1,0:T(8,128)(2,1)S(1)}, bf16[256,256]{1,0:T(8,128)(2,1)}, u32[]{:S(2)}) copy-start(bf16[256,256]{1,0:T(8,128)(2,1)} %refs_2_.1) | copy-start | bytes 393220
  95.2 6.0 %copy-start.5 = (bf16[256,256]{1,0:T(8,128)(2,1)S(1)}, bf16[256,256]{1,0:T(8,128)(2,1)}, u32[]{:S(2)}) copy-start(bf16[256,256]{1,0:T(8,128)(2,1)} %refs_3_.1) | copy-start | bytes 393220
  95.2 47.7 %all-to-all-start.1 = ((bf16[16,768,128]{2,1,0:T(8,128)(2,1)}), bf16[16,768,128]{2,1,0:T(8,128)(2,1)}, u32[]{:S(2)}, u32[]{:S(2)}) async-start(bf16[16,768,128]{2,1,0:T(8,128)(2,1)} %bitcast.57), calls=%async_computation.1 | async-start | bytes 6291456 | tf_op jit(solution)/shard_map/all_to_all | solution.py:352
  127.7 2.5 %collective-permute-start.8 = (bf16[4,160,512]{2,1,0:T(8,128)(2,1)}, bf16[4,160,512]{2,1,0:T(8,128)(2,1)S(1)}, u32[]{:S(2)}, u32[]{:S(2)}) collective-permute-start(bf16[4,160,512]{2,1,0:T(8,128)(2,1)} %get-tuple-element.48), channel_id=1, source_target_pairs={{0,8},{1,9},{2,10},{3,11},{4,12},{5,13},{6,14},{7,15},{8,0},{9,1},... | collective-permute-start | bytes 1966088 | tf_op jit(solution)/shard_map/ppermute | solution.py:301
  129.0 6.5 %collective-permute-start.12 = (bf16[24,512]{1,0:T(8,128)(2,1)S(1)}, bf16[24,512]{1,0:T(8,128)(2,1)S(1)}, u32[]{:S(2)}, u32[]{:S(2)}) collective-permute-start(bf16[24,512]{1,0:T(8,128)(2,1)S(1)} %convert_element_type.91), channel_id=1, source_target_pairs={{0,8},{1,9},{2,10},{3,11},{4,12},{5,13},{6,14},{7,15},{8,0},{9,1},... | collective-permute-start | bytes 73736 | tf_op jit(solution)/shard_map/ppermute | solution.py:301
  130.2 5.4 %copy-start.3 = (f32[24,512]{1,0:T(8,128)S(1)}, f32[24,512]{1,0:T(8,128)}, u32[]{:S(2)}) copy-start(f32[24,512]{1,0:T(8,128)} %get-tuple-element.49) | copy-start | bytes 147460
  131.8 7.1 %collective-permute-start.10 = (bf16[160,512]{1,0:T(8,128)(2,1)S(1)}, bf16[160,512]{1,0:T(8,128)(2,1)S(1)}, u32[]{:S(2)}, u32[]{:S(2)}) collective-permute-start(bf16[160,512]{1,0:T(8,128)(2,1)S(1)} %get-tuple-element.86), channel_id=1, source_target_pairs={{0,2},{1,3},{2,0},{3,1},{4,6},{5,7},{6,4},{7,5},{8,10},{9,11},{10,... | collective-permute-start | bytes 491528 | tf_op jit(solution)/shard_map/ppermute | solution.py:301
  134.8 8.1 %collective-permute-start.11 = (bf16[160,512]{1,0:T(8,128)(2,1)S(1)}, bf16[160,512]{1,0:T(8,128)(2,1)S(1)}, u32[]{:S(2)}, u32[]{:S(2)}) collective-permute-start(bf16[160,512]{1,0:T(8,128)(2,1)S(1)} %get-tuple-element.85), channel_id=1, source_target_pairs={{0,3},{1,2},{2,1},{3,0},{4,7},{5,6},{6,5},{7,4},{8,11},{9,10},{10,... | collective-permute-start | bytes 491528 | tf_op jit(solution)/shard_map/ppermute | solution.py:301
  135.5 7.3 %collective-permute-start.9 = (bf16[160,512]{1,0:T(8,128)(2,1)S(1)}, bf16[160,512]{1,0:T(8,128)(2,1)S(1)}, u32[]{:S(2)}, u32[]{:S(2)}) collective-permute-start(bf16[160,512]{1,0:T(8,128)(2,1)S(1)} %get-tuple-element.84), channel_id=1, source_target_pairs={{0,1},{1,0},{2,3},{3,2},{4,5},{5,4},{6,7},{7,6},{8,9},{9,8},{10,11... | collective-permute-start | bytes 491528 | tf_op jit(solution)/shard_map/ppermute | solution.py:301
  143.0 5.8 %collective-permute-start.13 = (bf16[208,512]{1,0:T(8,128)(2,1)S(1)}, bf16[208,512]{1,0:T(8,128)(2,1)S(1)}, u32[]{:S(2)}, u32[]{:S(2)}) collective-permute-start(bf16[208,512]{1,0:T(8,128)(2,1)S(1)} %pad_maximum_fusion.9), channel_id=1, source_target_pairs={{0,32},{1,33},{2,34},{3,35},{4,36},{5,37},{6,38},{7,39},{8,40},{9,... | collective-permute-start | bytes 638984 | tf_op jit(solution)/shard_map/ppermute | solution.py:301
  144.4 6.7 %collective-permute-start.15 = (bf16[208,512]{1,0:T(8,128)(2,1)S(1)}, bf16[208,512]{1,0:T(8,128)(2,1)S(1)}, u32[]{:S(2)}, u32[]{:S(2)}) collective-permute-start(bf16[208,512]{1,0:T(8,128)(2,1)S(1)} %pad_maximum_fusion.9), channel_id=1, source_target_pairs={{0,96},{1,97},{2,98},{3,99},{4,100},{5,101},{6,102},{7,103},{8,104... | collective-permute-start | bytes 638984 | tf_op jit(solution)/shard_map/ppermute | solution.py:301
  146.2 9.6 %collective-permute-start.14 = (bf16[208,512]{1,0:T(8,128)(2,1)S(1)}, bf16[208,512]{1,0:T(8,128)(2,1)S(1)}, u32[]{:S(2)}, u32[]{:S(2)}) collective-permute-start(bf16[208,512]{1,0:T(8,128)(2,1)S(1)} %pad_maximum_fusion.9), channel_id=1, source_target_pairs={{0,64},{1,65},{2,66},{3,67},{4,68},{5,69},{6,70},{7,71},{8,72},{9,... | collective-permute-start | bytes 638984 | tf_op jit(solution)/shard_map/ppermute | solution.py:301
  156.0 9.5 %collective-permute-start.17 = (bf16[352,512]{1,0:T(8,128)(2,1)S(1)}, bf16[352,512]{1,0:T(8,128)(2,1)S(1)}, u32[]{:S(2)}, u32[]{:S(2)}) collective-permute-start(bf16[352,512]{1,0:T(8,128)(2,1)S(1)} %pad_maximum_fusion.8), channel_id=1, source_target_pairs={{0,16},{1,17},{2,18},{3,19},{4,20},{5,21},{6,22},{7,23},{8,24},{9,... | collective-permute-start | bytes 1081352 | tf_op jit(solution)/shard_map/ppermute | solution.py:301
  158.7 10.7 %collective-permute-start.16 = (bf16[160,512]{1,0:T(8,128)(2,1)S(1)}, bf16[160,512]{1,0:T(8,128)(2,1)S(1)}, u32[]{:S(2)}, u32[]{:S(2)}) collective-permute-start(bf16[160,512]{1,0:T(8,128)(2,1)S(1)} %add_convert_fusion.1), channel_id=1, source_target_pairs={{0,4},{1,5},{2,6},{3,7},{4,0},{5,1},{6,2},{7,3},{8,12},{9,13},{10,... | collective-permute-start | bytes 491528 | tf_op jit(solution)/shard_map/ppermute | solution.py:301
  159.5 11.4 %collective-permute-start.18 = (bf16[160,512]{1,0:T(8,128)(2,1)S(1)}, bf16[160,512]{1,0:T(8,128)(2,1)S(1)}, u32[]{:S(2)}, u32[]{:S(2)}) collective-permute-start(bf16[160,512]{1,0:T(8,128)(2,1)S(1)} %add_convert_fusion.1), channel_id=1, source_target_pairs={{0,20},{1,21},{2,22},{3,23},{4,16},{5,17},{6,18},{7,19},{8,28},{9,... | collective-permute-start | bytes 491528 | tf_op jit(solution)/shard_map/ppermute | solution.py:301
  171.0 46.7 %all-to-all-start.2 = ((bf16[16,768,128]{2,1,0:T(8,128)(2,1)}), bf16[16,768,128]{2,1,0:T(8,128)(2,1)}, u32[]{:S(2)}, u32[]{:S(2)}) async-start(bf16[16,768,128]{2,1,0:T(8,128)(2,1)} %bitcast.25), calls=%async_computation.2 | async-start | bytes 6291456 | tf_op jit(solution)/shard_map/all_to_all | solution.py:352
  177.8 5.7 %collective-permute-start.19 = (bf16[160,512]{1,0:T(8,128)(2,1)S(1)}, bf16[160,512]{1,0:T(8,128)(2,1)S(1)}, u32[]{:S(2)}, u32[]{:S(2)}) collective-permute-start(bf16[160,512]{1,0:T(8,128)(2,1)S(1)} %add_convert_fusion), channel_id=1, source_target_pairs={{0,1},{1,0},{2,3},{3,2},{4,5},{5,4},{6,7},{7,6},{8,9},{9,8},{10,11... | collective-permute-start | bytes 491528 | tf_op jit(solution)/shard_map/ppermute | solution.py:301
  179.1 10.4 %collective-permute-start.20 = (bf16[160,512]{1,0:T(8,128)(2,1)S(1)}, bf16[160,512]{1,0:T(8,128)(2,1)S(1)}, u32[]{:S(2)}, u32[]{:S(2)}) collective-permute-start(bf16[160,512]{1,0:T(8,128)(2,1)S(1)} %add_convert_fusion), channel_id=1, source_target_pairs={{0,2},{1,3},{2,0},{3,1},{4,6},{5,7},{6,4},{7,5},{8,10},{9,11},{10,... | collective-permute-start | bytes 491528 | tf_op jit(solution)/shard_map/ppermute | solution.py:301
  181.7 10.3 %collective-permute-start.21 = (bf16[160,512]{1,0:T(8,128)(2,1)S(1)}, bf16[160,512]{1,0:T(8,128)(2,1)S(1)}, u32[]{:S(2)}, u32[]{:S(2)}) collective-permute-start(bf16[160,512]{1,0:T(8,128)(2,1)S(1)} %add_convert_fusion), channel_id=1, source_target_pairs={{0,3},{1,2},{2,1},{3,0},{4,7},{5,6},{6,5},{7,4},{8,11},{9,10},{10,... | collective-permute-start | bytes 491528 | tf_op jit(solution)/shard_map/ppermute | solution.py:301
  193.0 9.7 %collective-permute-start.22 = (bf16[4,160,512]{2,1,0:T(8,128)(2,1)}, bf16[4,160,512]{2,1,0:T(8,128)(2,1)}, u32[]{:S(2)}, u32[]{:S(2)}) collective-permute-start(bf16[4,160,512]{2,1,0:T(8,128)(2,1)} %bitcast.32), channel_id=1, source_target_pairs={{0,8},{1,9},{2,10},{3,11},{4,12},{5,13},{6,14},{7,15},{8,0},{9,1},... | collective-permute-start | bytes 1966088 | tf_op jit(solution)/shard_map/ppermute | solution.py:301
  217.7 3.6 %copy-start.1 = (f32[192,512]{1,0:T(8,128)S(1)}, f32[192,512]{1,0:T(8,128)}, u32[]{:S(2)}) copy-start(f32[192,512]{1,0:T(8,128)} %param.16) | copy-start | bytes 1179652
  (2 other events, 4.1 us)

commit v3 on v2

--- a/solution.py
+++ b/solution.py
@@ -23,7 +23,7 @@
 STEPS = WIDTH // BLOCK
 PIECES = 8
 FINAL_BLOCK = 48
-FORWARD_GROUP = 6
+FORWARD_GROUP = 3
 BACKWARD_GROUP = 3
 SUM_ROWS = 2 * OWNED
 HIGH_ONE = P2 // PIECES
@@ -147,17 +147,24 @@
     )(h, g, four)
 
 
-def forward_kernel(x_ref, one_ref, two_ref, three_ref, kc_ref, kr_ref, h_ref):
+def forward_kernel(
+    x_ref, one_ref, two_ref, three_ref, kc_ref, kr_ref, h_ref, first_ref, left_ref
+):
     for q in range(FORWARD_GROUP):
         x = from_slabs(x_ref, (q,)).reshape(P1, P2)
-        first = (nn(x, one_ref[...]) * kc_ref[q]).astype(half)
-        left = (nn(two_ref[...], first) * kr_ref[q]).astype(half)
+        first_prod = nn(x, one_ref[...])
+        first_ref[q] = first_prod
+        first = (first_prod * kc_ref[q]).astype(half)
+        left_prod = nn(two_ref[...], first)
+        left_ref[q] = left_prod
+        left = (left_prod * kr_ref[q]).astype(half)
         second = nn(three_ref[...], left).astype(half)
         to_slabs(second.reshape(N_SEQ, ROWS, P2), h_ref, (q,))
 
 
 def backward_channels(e_ref, refs, accs, dx_ref, sums_ref):
-    x_ref, one_ref, two_ref, three_ref, four_ref, two_t_ref, three_t_ref, kc_ref, kr_ref = refs
+    x_ref, h_ref, first_ref, left_ref, one_ref, four_ref, two_t_ref, three_t_ref = refs[:8]
+    kc_ref, kr_ref = refs[8:]
     acc_one, acc_two, acc_three, acc_four = accs
     step = pl.program_id(0)
     for q in range(BACKWARD_GROUP):
@@ -165,11 +172,11 @@
         kr = kr_ref[q]
         x = from_slabs(x_ref, (q,)).reshape(P1, P2)
         e = from_slabs(e_ref, (q,)).reshape(P1, P2)
-        first_prod = nn(x, one_ref[...])
+        second = from_slabs(h_ref, (q,)).reshape(P1, P2)
+        first_prod = first_ref[q]
         first = (first_prod * kc).astype(half)
-        left_prod = nn(two_ref[...], first)
+        left_prod = left_ref[q]
         left = (left_prod * kr).astype(half)
-        second = nn(three_ref[...], left).astype(half)
         d_second = nt(e, four_ref[...]).astype(half)
         d_left = nn(three_t_ref[...], d_second)
         row_terms = d_left * left_prod
@@ -191,8 +198,8 @@
 
 
 def backward_kernel(*refs):
-    e_parts = refs[9 : 9 + N_CHIP]
-    dx_ref, sums_ref, keep_ref, send_ref, *accs, e_ref = refs[9 + N_CHIP :]
+    e_parts = refs[10 : 10 + N_CHIP]
+    dx_ref, sums_ref, keep_ref, send_ref, *accs, e_ref = refs[10 + N_CHIP :]
     step = pl.program_id(0)
     seq = lax.axis_index("seq")
     for offset, ref in zip(MESSAGE_ORDER, e_parts):
@@ -205,7 +212,7 @@
         for ref in (*accs, sums_ref):
             ref[...] = jnp.zeros_like(ref)
 
-    backward_channels(e_ref, refs[:9], accs, dx_ref, sums_ref)
+    backward_channels(e_ref, refs[:10], accs, dx_ref, sums_ref)
     core = seq % 2
     acc_one, acc_two, acc_three, acc_four = accs
 
@@ -237,6 +244,10 @@
     return pl.BlockSpec((N_SEQ, n, HEIGHT, 128), lambda q: (0, q, 0, 0))
 
 
+def mat(n):
+    return pl.BlockSpec((n, P1, P2), lambda q: (q, 0, 0))
+
+
 def col(n):
     return pl.BlockSpec((n, 1, P2), lambda q: (q, 0, 0))
 
@@ -246,6 +257,7 @@
 
 
 OWN_SHAPE = jax.ShapeDtypeStruct((N_SEQ, OWNED, HEIGHT, 128), half)
+MAT_SHAPE = jax.ShapeDtypeStruct((OWNED, P1, P2), flt)
 BIG = 2 * P1 * P2 * P2 * OWNED
 SMALL = 2 * P1 * P1 * P2 * OWNED
 
@@ -255,8 +267,9 @@
     return pl.pallas_call(
         forward_kernel, grid=(OWNED // n,),
         in_specs=[own(n), whole(P2, P2), whole(P1, P1), whole(P1, P1), col(n), row(n)],
-        out_specs=own(n), out_shape=OWN_SHAPE, compiler_params=params(),
-        cost_estimate=cost(BIG + 2 * SMALL, 2 * SIZE), name="forward_owned",
+        out_specs=[own(n), mat(n), mat(n)], out_shape=[OWN_SHAPE, MAT_SHAPE, MAT_SHAPE],
+        compiler_params=params(), cost_estimate=cost(BIG + 2 * SMALL, 6 * SIZE),
+        name="forward_owned",
     )(x, one, two, three, kc, kr)
 
 
@@ -269,7 +282,7 @@
     return pl.pallas_call(
         backward_kernel, grid=(OWNED // n,),
         in_specs=[
-            own(n), whole(P2, P2), whole(P1, P1), whole(P1, P1), whole(P2, P2),
+            own(n), own(n), mat(n), mat(n), whole(P2, P2), whole(P2, P2),
             whole(P1, P1), whole(P1, P1), col(n), row(n),
         ]
         + [pl.BlockSpec((2, n, HEIGHT, 128), lambda q: (0, q, 0, 0))] * N_CHIP,
@@ -283,7 +296,7 @@
             pltpu.VMEM((N_SEQ, n, HEIGHT, 128), half),
         ],
         compiler_params=params(),
-        cost_estimate=cost(5 * BIG + 6 * SMALL, 3 * SIZE), name="backward_owned",
+        cost_estimate=cost(4 * BIG + 4 * SMALL, 8 * SIZE), name="backward_owned",
     )(*args, *e_parts)
 
 
@@ -384,14 +397,12 @@
 
     x_own = exchange(split(inputs)).reshape(owned)
     e_parts = exchange_by_chip(*gate(upstream, gating), seq >> 1)
-    h_own = forward(x_own, factor_one, factor_two, factor_three, kc, kr)
-    h_own, *e_parts = after(h_own, *e_parts)
+    h_own, first, left = forward(x_own, factor_one, factor_two, factor_three, kc, kr)
+    *arrived, last = e_parts
+    h_own, two_t, three_t, *arrived = after(h_own, factor_two.T, factor_three.T, *arrived)
     h_rows = exchange(h_own).reshape(by_channel)
-    args = (
-        x_own, factor_one, factor_two, factor_three, factor_four, factor_two.T, factor_three.T,
-        kc, kr,
-    )
-    dx_own, sums, keep, send = backward(args, e_parts)
+    args = (x_own, h_own, first, left, factor_one, factor_four, two_t, three_t, kc, kr)
+    dx_own, sums, keep, send = backward(args, (*arrived, last))
     sums = sums.astype(half)
     sums = in_order(core_at, sums, swap(sums, core=1)).reshape(2 * SUM_ROWS, P2)
     mine = reduce_grads(keep, send, y_at)

time: 224 us -> 215 us (0.960)
  waiting for transfers between devices: 89.4 us -> 79.2 us
  Pallas kernels: 55.5 us -> 51.5 us
  starting transfers between devices: 55.4 us -> 58.3 us
  local copies, waits for them, and re-layouts: 8.09 us -> 10.7 us
    ppermute x23, waiting for transfers between devices: 79.4 us -> 69 us  [swap(): return lax.ppermute(v, AXES, swap_pairs(**flips))]
    pallas_call x1, Pallas kernels: 25.7 us -> 20.5 us  [backward(): pl.pallas_call(backward_kernel, grid=(OWNED // n,), in_specs=[own(n), own...]
    ppermute x23, starting transfers between devices: 34.2 us -> 37.4 us  [swap(): return lax.ppermute(v, AXES, swap_pairs(**flips))]
    unnamed x18 -> x16, local copies, waits for them, and re-layouts: 2.23 us -> 4.85 us
  transfers between devices with their start and end apart: 26 -> 26, of which waited for: 17 -> 16; matrix products, arithmetic and copies ran while one was open for 9% -> 10% of each run, Pallas kernels for 22% -> 21%
where the time goes in v3:
time: 215 us; the launch traced here: 213 us
  waiting for transfers between devices  79.2 us (37%)
  starting transfers between devices  58.3 us (27%)
  Pallas kernels  51.5 us (24%)
  other arithmetic  11.9 us (6%)
  local copies, waits for them, and re-layouts  10.7 us (5%)
    ppermute x23, waiting for transfers between devices, swap(): return lax.ppermute(v, AXES, swap_pairs(**flips))  69 us
    ppermute x23, starting transfers between devices, swap(): return lax.ppermute(v, AXES, swap_pairs(**flips))  37.4 us
    all_to_all x3, starting transfers between devices, exchange(): return lax.all_to_all(rows, 'seq', split_axis=0, concat_axis=0, tiled=True)  20.9 us
    pallas_call x1, Pallas kernels, backward(): pl.pallas_call(backward_kernel, grid=(OWNED // n,), in_specs=[own(n), own...  20.5 us
    pallas_call x1, Pallas kernels, forward(): pl.pallas_call(forward_kernel, grid=(OWNED // n,), in_specs=[own(n), whol...  11.1 us
    all_to_all x3, waiting for transfers between devices, exchange(): return lax.all_to_all(rows, 'seq', split_axis=0, concat_axis=0, tiled=True)  10.1 us
    pallas_call x1, Pallas kernels, final(): pl.pallas_call(final_kernel, grid=(WIDTH // FINAL_BLOCK,), in_specs=[mats...  7.02 us
    pallas_call x1, Pallas kernels, gate(): pl.pallas_call(gate_kernel, grid=(STEPS,), in_specs=[flat(BLOCK), flat(BL...  5.74 us
  transfers between devices with their start and end apart: 26, of which 16 were waited for; matrix products, arithmetic and copies ran while one was open for 10% of the time, Pallas kernels for 21%

profile of v3, /device:TPU:1, one launch (start us, length us, event | category | flops | bytes accessed | tf_op | source)
XLA Modules:
  0.0 212.6 jit_solution(5477831842182574252)
XLA Ops:
  0.6 3.6 %split_rows.1 = bf16[192,64,128]{2,1,0:T(8,128)(2,1)} custom-call(bf16[192,8192]{1,0:T(8,128)(2,1)} %x_ref.1), custom_call_target="tpu_custom_call" | custom-call | bytes 6291456 | tf_op jit(solution)/shard_map/split_rows/pallas_call | solution.py:118
  4.3 9.1 %all-to-all-start = ((bf16[16,768,128]{2,1,0:T(8,128)(2,1)}), bf16[16,768,128]{2,1,0:T(8,128)(2,1)}, u32[]{:S(2)}, u32[]{:S(2)}) async-start(bf16[16,768,128]{2,1,0:T(8,128)(2,1)} %bitcast.56), calls=%async_computation | async-start | bytes 6291456 | tf_op jit(solution)/shard_map/all_to_all | solution.py:365
  13.4 5.7 %gate_rows.1 = (bf16[8,12,64,128]{3,2,1,0:T(8,128)(2,1)}, bf16[8,12,64,128]{3,2,1,0:T(8,128)(2,1)}) custom-call(bf16[192,8192]{1,0:T(8,128)(2,1)} %g_ref.3, bf16[192,8192]{1,0:T(8,128)(2,1)} %z_ref.1), custom_call_target="tpu_custom_call" | custom-call | bytes 9437184 | tf_op jit(solution)/shard_map/gate_rows/pallas_call | solution.py:127
  27.9 1.9 collective-permute-start.2
  29.8 2.8 %collective-permute-start.3 = (bf16[2,12,64,128]{3,2,1,0:T(8,128)(2,1)S(1)}, bf16[2,12,64,128]{3,2,1,0:T(8,128)(2,1)}, u32[]{:S(2)}, u32[]{:S(2)}) collective-permute-start(bf16[2,12,64,128]{3,2,1,0:T(8,128)(2,1)S(1)} %pad_maximum_fusion.3), channel_id=1, source_target_pairs={{0,48},{1,49},{2,50},{3,51},{4,52},{5,53},{6,54},{7,55},{8,56},{9,... | collective-permute-start | bytes 1179656 | tf_op jit(solution)/shard_map/ppermute | solution.py:314
  34.8 2.7 %collective-permute-start.5 = (bf16[2,12,64,128]{3,2,1,0:T(8,128)(2,1)}, bf16[2,12,64,128]{3,2,1,0:T(8,128)(2,1)}, u32[]{:S(2)}, u32[]{:S(2)}) collective-permute-start(bf16[2,12,64,128]{3,2,1,0:T(8,128)(2,1)} %pad_maximum_fusion.5), channel_id=1, source_target_pairs={{0,16},{1,17},{2,18},{3,19},{4,20},{5,21},{6,22},{7,23},{8,24},{9,... | collective-permute-start | bytes 1179656 | tf_op jit(solution)/shard_map/ppermute | solution.py:314
  39.0 20.1 %collective-permute-done.1.refs_11_ = bf16[2,12,64,128]{3,2,1,0:T(8,128)(2,1)S(1)} collective-permute-done((bf16[2,12,64,128]{3,2,1,0:T(8,128)(2,1)S(1)}, bf16[2,12,64,128]{3,2,1,0:T(8,128)(2,1)S(1)}, u32[]{:S(2)}, u32[]{:S(2)}) %collective-permute-start.1) | collective-permute-done | bytes 393248 | tf_op jit(solution)/shard_map/ppermute | solution.py:314
  59.1 7.8 %collective-permute-start.6 = (bf16[2,12,64,128]{3,2,1,0:T(8,128)(2,1)}, bf16[2,12,64,128]{3,2,1,0:T(8,128)(2,1)}, u32[]{:S(2)}, u32[]{:S(2)}) collective-permute-start(bf16[2,12,64,128]{3,2,1,0:T(8,128)(2,1)} %pad_maximum_fusion.6), channel_id=1, source_target_pairs={{0,64},{1,65},{2,66},{3,67},{4,68},{5,69},{6,70},{7,71},{8,72},{9,... | collective-permute-start | bytes 1179656 | tf_op jit(solution)/shard_map/ppermute | solution.py:314
  68.5 11.1 %forward_owned.1 = (bf16[16,12,64,128]{3,2,1,0:T(8,128)(2,1)}, f32[12,256,512]{2,1,0:T(8,128)}, f32[12,256,512]{2,1,0:T(8,128)}) custom-call(bf16[16,12,64,128]{3,2,1,0:T(8,128)(2,1)} %bitcast.1.x_ref.refs_0_, bf16[512,512]{1,0:T(8,128)(2,1)} %refs_4_.1, bf16[256,256]{1,0:T(8,128)(2,1)} %two_ref.1, bf16[256,256]{1,0:T(8,128)(2,1)} %three_ref.1, ...), custom_call_target="tpu_custom_call" | custom-call | flops 3221225472 | bytes 18874368 | tf_op jit(solution)/shard_map/forward_owned/pallas_call | solution.py:267
  79.6 6.4 %collective-permute-done.6.refs_16_ = bf16[2,12,64,128]{3,2,1,0:T(8,128)(2,1)} collective-permute-done((bf16[2,12,64,128]{3,2,1,0:T(8,128)(2,1)}, bf16[2,12,64,128]{3,2,1,0:T(8,128)(2,1)}, u32[]{:S(2)}, u32[]{:S(2)}) %collective-permute-start.6) | collective-permute-done | bytes 393248 | tf_op jit(solution)/shard_map/ppermute | solution.py:314
  86.0 5.9 %all-to-all-start.1 = ((bf16[16,768,128]{2,1,0:T(8,128)(2,1)}), bf16[16,768,128]{2,1,0:T(8,128)(2,1)}, u32[]{:S(2)}, u32[]{:S(2)}) async-start(bf16[16,768,128]{2,1,0:T(8,128)(2,1)} %bitcast.57), calls=%async_computation.1 | async-start | bytes 6291456 | tf_op jit(solution)/shard_map/all_to_all | solution.py:365
  91.9 3.2 %collective-permute-done.7.refs_17_ = bf16[2,12,64,128]{3,2,1,0:T(8,128)(2,1)S(1)} collective-permute-done((bf16[2,12,64,128]{3,2,1,0:T(8,128)(2,1)}, bf16[2,12,64,128]{3,2,1,0:T(8,128)(2,1)S(1)}, u32[]{:S(2)}, u32[]{:S(2)}) %collective-permute-start.7) | collective-permute-done | bytes 393248 | tf_op jit(solution)/shard_map/ppermute | solution.py:314
  95.9 20.5 %backward_owned.1 = (bf16[16,12,64,128]{3,2,1,0:T(8,128)(2,1)}, f32[24,512]{1,0:T(8,128)}, f32[4,160,512]{2,1,0:T(8,128)}, bf16[4,160,512]{2,1,0:T(8,128)(2,1)}) custom-call(bf16[16,12,64,128]{3,2,1,0:T(8,128)(2,1)} %bitcast.1.x_ref.refs_0_, bf16[16,12,64,128]{3,2,1,0:T(8,128)(2,1)} %get-tuple-element.44.refs_1_, f32[12,256,512]{2,1,0:T(8,128)} %get-tuple-element.45.refs_2_, ...), custom_call_target="tpu_custom_call" | custom-call | flops 9663676416 | bytes 25165824 | tf_op jit(solution)/shard_map/backward_owned/pallas_call | solution.py:282
  120.8 3.0 %collective-permute-start.10 = (bf16[160,512]{1,0:T(8,128)(2,1)S(1)}, bf16[160,512]{1,0:T(8,128)(2,1)S(1)}, u32[]{:S(2)}, u32[]{:S(2)}) collective-permute-start(bf16[160,512]{1,0:T(8,128)(2,1)S(1)} %get-tuple-element.94), channel_id=1, source_target_pairs={{0,2},{1,3},{2,0},{3,1},{4,6},{5,7},{6,4},{7,5},{8,10},{9,11},{10,... | collective-permute-start | bytes 491528 | tf_op jit(solution)/shard_map/ppermute | solution.py:314
  124.6 3.3 %collective-permute-done.10 = bf16[160,512]{1,0:T(8,128)(2,1)S(1)} collective-permute-done((bf16[160,512]{1,0:T(8,128)(2,1)S(1)}, bf16[160,512]{1,0:T(8,128)(2,1)S(1)}, u32[]{:S(2)}, u32[]{:S(2)}) %collective-permute-start.10) | collective-permute-done | bytes 163872 | tf_op jit(solution)/shard_map/ppermute | solution.py:314
  127.9 4.1 %collective-permute-done.11 = bf16[160,512]{1,0:T(8,128)(2,1)S(1)} collective-permute-done((bf16[160,512]{1,0:T(8,128)(2,1)S(1)}, bf16[160,512]{1,0:T(8,128)(2,1)S(1)}, u32[]{:S(2)}, u32[]{:S(2)}) %collective-permute-start.11) | collective-permute-done | bytes 163872 | tf_op jit(solution)/shard_map/ppermute | solution.py:314
  132.3 2.8 %collective-permute-start.15 = (bf16[208,512]{1,0:T(8,128)(2,1)S(1)}, bf16[208,512]{1,0:T(8,128)(2,1)S(1)}, u32[]{:S(2)}, u32[]{:S(2)}) collective-permute-start(bf16[208,512]{1,0:T(8,128)(2,1)S(1)} %pad_maximum_fusion.9), channel_id=1, source_target_pairs={{0,96},{1,97},{2,98},{3,99},{4,100},{5,101},{6,102},{7,103},{8,104... | collective-permute-start | bytes 638984 | tf_op jit(solution)/shard_map/ppermute | solution.py:314
  136.2 1.9 collective-permute-done.13
  138.1 1.9 collective-permute-done.15
  140.0 5.2 %collective-permute-done.14 = bf16[208,512]{1,0:T(8,128)(2,1)S(1)} collective-permute-done((bf16[208,512]{1,0:T(8,128)(2,1)S(1)}, bf16[208,512]{1,0:T(8,128)(2,1)S(1)}, u32[]{:S(2)}, u32[]{:S(2)}) %collective-permute-start.14) | collective-permute-done | bytes 213024 | tf_op jit(solution)/shard_map/ppermute | solution.py:314
  145.3 5.5 %collective-permute-start.17 = (bf16[352,512]{1,0:T(8,128)(2,1)S(1)}, bf16[352,512]{1,0:T(8,128)(2,1)S(1)}, u32[]{:S(2)}, u32[]{:S(2)}) collective-permute-start(bf16[352,512]{1,0:T(8,128)(2,1)S(1)} %pad_maximum_fusion.8), channel_id=1, source_target_pairs={{0,16},{1,17},{2,18},{3,19},{4,20},{5,21},{6,22},{7,23},{8,24},{9,... | collective-permute-start | bytes 1081352 | tf_op jit(solution)/shard_map/ppermute | solution.py:314
  151.6 7.0 %collective-permute-done.17 = bf16[352,512]{1,0:T(8,128)(2,1)S(1)} collective-permute-done((bf16[352,512]{1,0:T(8,128)(2,1)S(1)}, bf16[352,512]{1,0:T(8,128)(2,1)S(1)}, u32[]{:S(2)}, u32[]{:S(2)}) %collective-permute-start.17) | collective-permute-done | bytes 360480 | tf_op jit(solution)/shard_map/ppermute | solution.py:314
  158.7 3.9 %collective-permute-done.16 = bf16[160,512]{1,0:T(8,128)(2,1)S(1)} collective-permute-done((bf16[160,512]{1,0:T(8,128)(2,1)S(1)}, bf16[160,512]{1,0:T(8,128)(2,1)S(1)}, u32[]{:S(2)}, u32[]{:S(2)}) %collective-permute-start.16) | collective-permute-done | bytes 163872 | tf_op jit(solution)/shard_map/ppermute | solution.py:314
  163.3 5.9 %all-to-all-start.2 = ((bf16[16,768,128]{2,1,0:T(8,128)(2,1)}), bf16[16,768,128]{2,1,0:T(8,128)(2,1)}, u32[]{:S(2)}, u32[]{:S(2)}) async-start(bf16[16,768,128]{2,1,0:T(8,128)(2,1)} %bitcast.25), calls=%async_computation.2 | async-start | bytes 6291456 | tf_op jit(solution)/shard_map/all_to_all | solution.py:365
  170.4 2.6 %collective-permute-start.20 = (bf16[160,512]{1,0:T(8,128)(2,1)S(1)}, bf16[160,512]{1,0:T(8,128)(2,1)S(1)}, u32[]{:S(2)}, u32[]{:S(2)}) collective-permute-start(bf16[160,512]{1,0:T(8,128)(2,1)S(1)} %add_convert_fusion), channel_id=1, source_target_pairs={{0,2},{1,3},{2,0},{3,1},{4,6},{5,7},{6,4},{7,5},{8,10},{9,11},{10,... | collective-permute-start | bytes 491528 | tf_op jit(solution)/shard_map/ppermute | solution.py:314
  173.1 1.8 collective-permute-done.19
  174.9 6.0 %collective-permute-done.20 = bf16[160,512]{1,0:T(8,128)(2,1)S(1)} collective-permute-done((bf16[160,512]{1,0:T(8,128)(2,1)S(1)}, bf16[160,512]{1,0:T(8,128)(2,1)S(1)}, u32[]{:S(2)}, u32[]{:S(2)}) %collective-permute-start.20) | collective-permute-done | bytes 163872 | tf_op jit(solution)/shard_map/ppermute | solution.py:314
  180.8 2.5 %collective-permute-done.21 = bf16[160,512]{1,0:T(8,128)(2,1)S(1)} collective-permute-done((bf16[160,512]{1,0:T(8,128)(2,1)S(1)}, bf16[160,512]{1,0:T(8,128)(2,1)S(1)}, u32[]{:S(2)}, u32[]{:S(2)}) %collective-permute-start.21) | collective-permute-done | bytes 163872 | tf_op jit(solution)/shard_map/ppermute | solution.py:314
  185.4 7.0 %final_rows.1 = bf16[192,8192]{1,0:T(8,128)(2,1)} custom-call(bf16[192,64,128]{2,1,0:T(8,128)(2,1)} %bitcast.13.h_ref, bf16[192,8192]{1,0:T(8,128)(2,1)} %g_ref.3, bf16[512,512]{1,0:T(8,128)(2,1)} %four_ref.1), custom_call_target="tpu_custom_call" | custom-call | flops 1610612736 | bytes 9437184 | tf_op jit(solution)/shard_map/final_rows/pallas_call | solution.py:142
  194.1 1.9 maximum_select_fusion
  198.9 10.1 %all-to-all-done.2 = bf16[16,768,128]{2,1,0:T(8,128)(2,1)} async-done(((bf16[16,768,128]{2,1,0:T(8,128)(2,1)}), bf16[16,768,128]{2,1,0:T(8,128)(2,1)}, u32[]{:S(2)}, u32[]{:S(2)}) %all-to-all-start.2) | async-done | bytes 3145760 | tf_op jit(solution)/shard_map/all_to_all | solution.py:365
  209.0 3.6 %join_rows.1 = bf16[192,8192]{1,0:T(8,128)(2,1)} custom-call(bf16[192,64,128]{2,1,0:T(8,128)(2,1)} %bitcast.26.x_ref), custom_call_target="tpu_custom_call" | custom-call | bytes 6291456 | tf_op jit(solution)/shard_map/join_rows/pallas_call | solution.py:135
  (87 shorter events, 31.0 us)
Async XLA Ops:
  0.6 21.2 %copy-start = (f32[192,512]{1,0:T(8,128)S(1)}, f32[192,512]{1,0:T(8,128)}, u32[]{:S(2)}) copy-start(f32[192,512]{1,0:T(8,128)} %param.16) | copy-start | bytes 1179652
  4.3 64.2 %all-to-all-start = ((bf16[16,768,128]{2,1,0:T(8,128)(2,1)}), bf16[16,768,128]{2,1,0:T(8,128)(2,1)}, u32[]{:S(2)}, u32[]{:S(2)}) async-start(bf16[16,768,128]{2,1,0:T(8,128)(2,1)} %bitcast.56), calls=%async_computation | async-start | bytes 6291456 | tf_op jit(solution)/shard_map/all_to_all | solution.py:365
  19.2 6.6 %copy-start.2 = (bf16[8,12,64,128]{3,2,1,0:T(8,128)(2,1)S(1)}, bf16[8,12,64,128]{3,2,1,0:T(8,128)(2,1)}, u32[]{:S(2)}) copy-start(bf16[8,12,64,128]{3,2,1,0:T(8,128)(2,1)} %get-tuple-element.42) | copy-start | bytes 4718596
  19.2 6.8 %collective-permute-start = (bf16[8,12,64,128]{3,2,1,0:T(8,128)(2,1)}, bf16[8,12,64,128]{3,2,1,0:T(8,128)(2,1)S(1)}, u32[]{:S(2)}, u32[]{:S(2)}) collective-permute-start(bf16[8,12,64,128]{3,2,1,0:T(8,128)(2,1)} %get-tuple-element.43), channel_id=1, source_target_pairs={{0,8},{1,9},{2,10},{3,11},{4,12},{5,13},{6,14},{7,15},{8,0},{9,1},... | collective-permute-start | bytes 4718600 | tf_op jit(solution)/shard_map/ppermute | solution.py:314
  26.2 32.9 %collective-permute-start.1 = (bf16[2,12,64,128]{3,2,1,0:T(8,128)(2,1)S(1)}, bf16[2,12,64,128]{3,2,1,0:T(8,128)(2,1)S(1)}, u32[]{:S(2)}, u32[]{:S(2)}) collective-permute-start(bf16[2,12,64,128]{3,2,1,0:T(8,128)(2,1)S(1)} %pad_maximum_fusion.1), channel_id=1, source_target_pairs={{0,32},{1,33},{2,34},{3,35},{4,36},{5,37},{6,38},{7,39},{8,40},{9,... | collective-permute-start | bytes 1179656 | tf_op jit(solution)/shard_map/ppermute | solution.py:314
  27.9 39.8 %collective-permute-start.2 = (bf16[2,12,64,128]{3,2,1,0:T(8,128)(2,1)S(1)}, bf16[2,12,64,128]{3,2,1,0:T(8,128)(2,1)S(1)}, u32[]{:S(2)}, u32[]{:S(2)}) collective-permute-start(bf16[2,12,64,128]{3,2,1,0:T(8,128)(2,1)S(1)} %pad_maximum_fusion.2), channel_id=1, source_target_pairs={{0,96},{1,97},{2,98},{3,99},{4,100},{5,101},{6,102},{7,103},{8,104... | collective-permute-start | bytes 1179656 | tf_op jit(solution)/shard_map/ppermute | solution.py:314
  29.8 49.8 %collective-permute-start.3 = (bf16[2,12,64,128]{3,2,1,0:T(8,128)(2,1)S(1)}, bf16[2,12,64,128]{3,2,1,0:T(8,128)(2,1)}, u32[]{:S(2)}, u32[]{:S(2)}) collective-permute-start(bf16[2,12,64,128]{3,2,1,0:T(8,128)(2,1)S(1)} %pad_maximum_fusion.3), channel_id=1, source_target_pairs={{0,48},{1,49},{2,50},{3,51},{4,52},{5,53},{6,54},{7,55},{8,56},{9,... | collective-permute-start | bytes 1179656 | tf_op jit(solution)/shard_map/ppermute | solution.py:314
  33.4 46.2 %collective-permute-start.4 = (bf16[2,12,64,128]{3,2,1,0:T(8,128)(2,1)}, bf16[2,12,64,128]{3,2,1,0:T(8,128)(2,1)}, u32[]{:S(2)}, u32[]{:S(2)}) collective-permute-start(bf16[2,12,64,128]{3,2,1,0:T(8,128)(2,1)} %pad_maximum_fusion.4), channel_id=1, source_target_pairs={{0,112},{1,113},{2,114},{3,115},{4,116},{5,117},{6,118},{7,119},{8... | collective-permute-start | bytes 1179656 | tf_op jit(solution)/shard_map/ppermute | solution.py:314
  34.8 44.8 %collective-permute-start.5 = (bf16[2,12,64,128]{3,2,1,0:T(8,128)(2,1)}, bf16[2,12,64,128]{3,2,1,0:T(8,128)(2,1)}, u32[]{:S(2)}, u32[]{:S(2)}) collective-permute-start(bf16[2,12,64,128]{3,2,1,0:T(8,128)(2,1)} %pad_maximum_fusion.5), channel_id=1, source_target_pairs={{0,16},{1,17},{2,18},{3,19},{4,20},{5,21},{6,22},{7,23},{8,24},{9,... | collective-permute-start | bytes 1179656 | tf_op jit(solution)/shard_map/ppermute | solution.py:314
  59.1 8.6 %copy-start.4 = (bf16[2,12,64,128]{3,2,1,0:T(8,128)(2,1)}, bf16[2,12,64,128]{3,2,1,0:T(8,128)(2,1)S(1)}, u32[]{:S(2)}) copy-start(bf16[2,12,64,128]{3,2,1,0:T(8,128)(2,1)S(1)} %collective-permute-done.1.refs_11_) | copy-start | bytes 1179652
  59.1 26.9 %collective-permute-start.6 = (bf16[2,12,64,128]{3,2,1,0:T(8,128)(2,1)}, bf16[2,12,64,128]{3,2,1,0:T(8,128)(2,1)}, u32[]{:S(2)}, u32[]{:S(2)}) collective-permute-start(bf16[2,12,64,128]{3,2,1,0:T(8,128)(2,1)} %pad_maximum_fusion.6), channel_id=1, source_target_pairs={{0,64},{1,65},{2,66},{3,67},{4,68},{5,69},{6,70},{7,71},{8,72},{9,... | collective-permute-start | bytes 1179656 | tf_op jit(solution)/shard_map/ppermute | solution.py:314
  67.7 0.8 copy-start.5
  68.5 26.6 %collective-permute-start.7 = (bf16[2,12,64,128]{3,2,1,0:T(8,128)(2,1)}, bf16[2,12,64,128]{3,2,1,0:T(8,128)(2,1)S(1)}, u32[]{:S(2)}, u32[]{:S(2)}) collective-permute-start(bf16[2,12,64,128]{3,2,1,0:T(8,128)(2,1)} %pad_maximum_fusion.7), channel_id=1, source_target_pairs={{0,80},{1,81},{2,82},{3,83},{4,84},{5,85},{6,86},{7,87},{8,88},{9,... | collective-permute-start | bytes 1179656 | tf_op jit(solution)/shard_map/ppermute | solution.py:314
  86.0 46.1 %all-to-all-start.1 = ((bf16[16,768,128]{2,1,0:T(8,128)(2,1)}), bf16[16,768,128]{2,1,0:T(8,128)(2,1)}, u32[]{:S(2)}, u32[]{:S(2)}) async-start(bf16[16,768,128]{2,1,0:T(8,128)(2,1)} %bitcast.57), calls=%async_computation.1 | async-start | bytes 6291456 | tf_op jit(solution)/shard_map/all_to_all | solution.py:365
  116.3 2.9 %collective-permute-start.8 = (bf16[4,160,512]{2,1,0:T(8,128)(2,1)}, bf16[4,160,512]{2,1,0:T(8,128)(2,1)S(1)}, u32[]{:S(2)}, u32[]{:S(2)}) collective-permute-start(bf16[4,160,512]{2,1,0:T(8,128)(2,1)} %get-tuple-element.57), channel_id=1, source_target_pairs={{0,8},{1,9},{2,10},{3,11},{4,12},{5,13},{6,14},{7,15},{8,0},{9,1},... | collective-permute-start | bytes 1966088 | tf_op jit(solution)/shard_map/ppermute | solution.py:314
  118.1 6.5 %collective-permute-start.12 = (bf16[24,512]{1,0:T(8,128)(2,1)S(1)}, bf16[24,512]{1,0:T(8,128)(2,1)S(1)}, u32[]{:S(2)}, u32[]{:S(2)}) collective-permute-start(bf16[24,512]{1,0:T(8,128)(2,1)S(1)} %convert_element_type.91), channel_id=1, source_target_pairs={{0,8},{1,9},{2,10},{3,11},{4,12},{5,13},{6,14},{7,15},{8,0},{9,1},... | collective-permute-start | bytes 73736 | tf_op jit(solution)/shard_map/ppermute | solution.py:314
  119.2 5.3 %copy-start.3 = (f32[24,512]{1,0:T(8,128)S(1)}, f32[24,512]{1,0:T(8,128)}, u32[]{:S(2)}) copy-start(f32[24,512]{1,0:T(8,128)} %get-tuple-element.58) | copy-start | bytes 147460
  120.8 7.1 %collective-permute-start.10 = (bf16[160,512]{1,0:T(8,128)(2,1)S(1)}, bf16[160,512]{1,0:T(8,128)(2,1)S(1)}, u32[]{:S(2)}, u32[]{:S(2)}) collective-permute-start(bf16[160,512]{1,0:T(8,128)(2,1)S(1)} %get-tuple-element.94), channel_id=1, source_target_pairs={{0,2},{1,3},{2,0},{3,1},{4,6},{5,7},{6,4},{7,5},{8,10},{9,11},{10,... | collective-permute-start | bytes 491528 | tf_op jit(solution)/shard_map/ppermute | solution.py:314
  123.8 8.2 %collective-permute-start.11 = (bf16[160,512]{1,0:T(8,128)(2,1)S(1)}, bf16[160,512]{1,0:T(8,128)(2,1)S(1)}, u32[]{:S(2)}, u32[]{:S(2)}) collective-permute-start(bf16[160,512]{1,0:T(8,128)(2,1)S(1)} %get-tuple-element.93), channel_id=1, source_target_pairs={{0,3},{1,2},{2,1},{3,0},{4,7},{5,6},{6,5},{7,4},{8,11},{9,10},{10,... | collective-permute-start | bytes 491528 | tf_op jit(solution)/shard_map/ppermute | solution.py:314
  124.6 7.5 %collective-permute-start.9 = (bf16[160,512]{1,0:T(8,128)(2,1)S(1)}, bf16[160,512]{1,0:T(8,128)(2,1)S(1)}, u32[]{:S(2)}, u32[]{:S(2)}) collective-permute-start(bf16[160,512]{1,0:T(8,128)(2,1)S(1)} %get-tuple-element.92), channel_id=1, source_target_pairs={{0,1},{1,0},{2,3},{3,2},{4,5},{5,4},{6,7},{7,6},{8,9},{9,8},{10,11... | collective-permute-start | bytes 491528 | tf_op jit(solution)/shard_map/ppermute | solution.py:314
  132.2 5.9 %collective-permute-start.13 = (bf16[208,512]{1,0:T(8,128)(2,1)S(1)}, bf16[208,512]{1,0:T(8,128)(2,1)S(1)}, u32[]{:S(2)}, u32[]{:S(2)}) collective-permute-start(bf16[208,512]{1,0:T(8,128)(2,1)S(1)} %pad_maximum_fusion.9), channel_id=1, source_target_pairs={{0,32},{1,33},{2,34},{3,35},{4,36},{5,37},{6,38},{7,39},{8,40},{9,... | collective-permute-start | bytes 638984 | tf_op jit(solution)/shard_map/ppermute | solution.py:314
  132.3 7.7 %collective-permute-start.15 = (bf16[208,512]{1,0:T(8,128)(2,1)S(1)}, bf16[208,512]{1,0:T(8,128)(2,1)S(1)}, u32[]{:S(2)}, u32[]{:S(2)}) collective-permute-start(bf16[208,512]{1,0:T(8,128)(2,1)S(1)} %pad_maximum_fusion.9), channel_id=1, source_target_pairs={{0,96},{1,97},{2,98},{3,99},{4,100},{5,101},{6,102},{7,103},{8,104... | collective-permute-start | bytes 638984 | tf_op jit(solution)/shard_map/ppermute | solution.py:314
  135.1 10.1 %collective-permute-start.14 = (bf16[208,512]{1,0:T(8,128)(2,1)S(1)}, bf16[208,512]{1,0:T(8,128)(2,1)S(1)}, u32[]{:S(2)}, u32[]{:S(2)}) collective-permute-start(bf16[208,512]{1,0:T(8,128)(2,1)S(1)} %pad_maximum_fusion.9), channel_id=1, source_target_pairs={{0,64},{1,65},{2,66},{3,67},{4,68},{5,69},{6,70},{7,71},{8,72},{9,... | collective-permute-start | bytes 638984 | tf_op jit(solution)/shard_map/ppermute | solution.py:314
  145.3 13.3 %collective-permute-start.17 = (bf16[352,512]{1,0:T(8,128)(2,1)S(1)}, bf16[352,512]{1,0:T(8,128)(2,1)S(1)}, u32[]{:S(2)}, u32[]{:S(2)}) collective-permute-start(bf16[352,512]{1,0:T(8,128)(2,1)S(1)} %pad_maximum_fusion.8), channel_id=1, source_target_pairs={{0,16},{1,17},{2,18},{3,19},{4,20},{5,21},{6,22},{7,23},{8,24},{9,... | collective-permute-start | bytes 1081352 | tf_op jit(solution)/shard_map/ppermute | solution.py:314
  150.8 11.7 %collective-permute-start.16 = (bf16[160,512]{1,0:T(8,128)(2,1)S(1)}, bf16[160,512]{1,0:T(8,128)(2,1)S(1)}, u32[]{:S(2)}, u32[]{:S(2)}) collective-permute-start(bf16[160,512]{1,0:T(8,128)(2,1)S(1)} %add_convert_fusion.1), channel_id=1, source_target_pairs={{0,4},{1,5},{2,6},{3,7},{4,0},{5,1},{6,2},{7,3},{8,12},{9,13},{10,... | collective-permute-start | bytes 491528 | tf_op jit(solution)/shard_map/ppermute | solution.py:314
  151.6 11.6 %collective-permute-start.18 = (bf16[160,512]{1,0:T(8,128)(2,1)S(1)}, bf16[160,512]{1,0:T(8,128)(2,1)S(1)}, u32[]{:S(2)}, u32[]{:S(2)}) collective-permute-start(bf16[160,512]{1,0:T(8,128)(2,1)S(1)} %add_convert_fusion.1), channel_id=1, source_target_pairs={{0,20},{1,21},{2,22},{3,23},{4,16},{5,17},{6,18},{7,19},{8,28},{9,... | collective-permute-start | bytes 491528 | tf_op jit(solution)/shard_map/ppermute | solution.py:314
  163.3 45.7 %all-to-all-start.2 = ((bf16[16,768,128]{2,1,0:T(8,128)(2,1)}), bf16[16,768,128]{2,1,0:T(8,128)(2,1)}, u32[]{:S(2)}, u32[]{:S(2)}) async-start(bf16[16,768,128]{2,1,0:T(8,128)(2,1)} %bitcast.25), calls=%async_computation.2 | async-start | bytes 6291456 | tf_op jit(solution)/shard_map/all_to_all | solution.py:365
  169.1 5.7 %collective-permute-start.19 = (bf16[160,512]{1,0:T(8,128)(2,1)S(1)}, bf16[160,512]{1,0:T(8,128)(2,1)S(1)}, u32[]{:S(2)}, u32[]{:S(2)}) collective-permute-start(bf16[160,512]{1,0:T(8,128)(2,1)S(1)} %add_convert_fusion), channel_id=1, source_target_pairs={{0,1},{1,0},{2,3},{3,2},{4,5},{5,4},{6,7},{7,6},{8,9},{9,8},{10,11... | collective-permute-start | bytes 491528 | tf_op jit(solution)/shard_map/ppermute | solution.py:314
  170.4 10.4 %collective-permute-start.20 = (bf16[160,512]{1,0:T(8,128)(2,1)S(1)}, bf16[160,512]{1,0:T(8,128)(2,1)S(1)}, u32[]{:S(2)}, u32[]{:S(2)}) collective-permute-start(bf16[160,512]{1,0:T(8,128)(2,1)S(1)} %add_convert_fusion), channel_id=1, source_target_pairs={{0,2},{1,3},{2,0},{3,1},{4,6},{5,7},{6,4},{7,5},{8,10},{9,11},{10,... | collective-permute-start | bytes 491528 | tf_op jit(solution)/shard_map/ppermute | solution.py:314
  173.1 10.3 %collective-permute-start.21 = (bf16[160,512]{1,0:T(8,128)(2,1)S(1)}, bf16[160,512]{1,0:T(8,128)(2,1)S(1)}, u32[]{:S(2)}, u32[]{:S(2)}) collective-permute-start(bf16[160,512]{1,0:T(8,128)(2,1)S(1)} %add_convert_fusion), channel_id=1, source_target_pairs={{0,3},{1,2},{2,1},{3,0},{4,7},{5,6},{6,5},{7,4},{8,11},{9,10},{10,... | collective-permute-start | bytes 491528 | tf_op jit(solution)/shard_map/ppermute | solution.py:314
  184.3 9.7 %collective-permute-start.22 = (bf16[4,160,512]{2,1,0:T(8,128)(2,1)}, bf16[4,160,512]{2,1,0:T(8,128)(2,1)}, u32[]{:S(2)}, u32[]{:S(2)}) collective-permute-start(bf16[4,160,512]{2,1,0:T(8,128)(2,1)} %bitcast.32), channel_id=1, source_target_pairs={{0,8},{1,9},{2,10},{3,11},{4,12},{5,13},{6,14},{7,15},{8,0},{9,1},... | collective-permute-start | bytes 1966088 | tf_op jit(solution)/shard_map/ppermute | solution.py:314
  209.0 3.6 %copy-start.1 = (f32[192,512]{1,0:T(8,128)S(1)}, f32[192,512]{1,0:T(8,128)}, u32[]{:S(2)}) copy-start(f32[192,512]{1,0:T(8,128)} %param.16) | copy-start | bytes 1179652
  (1 other events, 0.7 us)
